TPU v7x, 32 devices: a whole 2x2x4 slice. The times are simulated.
32 devices in a mesh: row: 4 (over y, x), col: 4 (over z), layer: 2 (over core).
Axes of the slice: x: 2, y: 2, z: 4, core: 2. Of those that a mesh axis runs over, the one named last changes fastest.
Arguments:
- tasks: bfloat16 [2048, 4096], P(('row', 'col')), may hold values from -0.25 to 0.25
- task_owner: int32 [2048, 1], P(('row', 'col')), may hold values from 0 to 15; in each aligned block of 128 rows (0 to 127, 128 to 255, ...) at most 16 rows name the same one
- task_slot: int32 [2048], P(('row', 'col')), may hold values from 0 to 63
- p_pattern: int32 [32, 32], P('row', 'col'), may hold values from 0 to 1, as said below
- c_pattern: int32 [32, 32], P('row', 'col'), may hold values from 0 to 1, as said below
- occupations: float32 [2048], P('row'), may hold values from 0.1 to 0.9
Outputs:
- purified: float32 [2048, 2048], P(('row', 'layer'), 'col')
Inputs may be any that keep to these rules, and one draw needn't show every extreme that they name: `task_owner`: the 128 tasks of one index of row and col name each owner at most 16 times. `task_slot`: a block of the owner's 8 x 8 blocks, row-major. `p_pattern`: 0 or 1; every diagonal block is 1. `c_pattern`: 0 or 1; every diagonal block is 1.
All inputs are finite; a program needn't handle non-finite values.
Results may differ from a plain program's by a relative error of at most 0.025.
Values may be sent and summed in bfloat16 or wider, within the bound.
No kernel may reach another device: no remote copies, remote signals or barrier semaphores. Data moves between devices by JAX's collectives and lax.ppermute only.
A program may use at most 64 MiB of HBM per device.

v0:
```python
import functools

import jax
import jax.numpy as jnp
from jax import lax
from jax.experimental import pallas as pl
from jax.experimental.pallas import tpu as pltpu
from jax.sharding import PartitionSpec as P

BLK = 64
LANES = 128
PACK_VMEM = 52 * 1024 * 1024
HEAVY = 10**10
EARLY = 0
EXTRA = 0
LATE = 0


def params(held):
    return pltpu.CompilerParams(vmem_limit_bytes=held + 6 * 1024 * 1024)


def whole_ref():
    return pl.BlockSpec(memory_space=pltpu.VMEM)


def any_ref():
    return pl.BlockSpec(memory_space=pl.ANY)


def cost(flops, bytes_accessed):
    return pl.CostEstimate(flops=flops, bytes_accessed=bytes_accessed, transcendentals=0)


def pack_kernel(owners, capacity, block_shape, paired, tasks_ref, owner_hbm, slot_hbm, *refs):
    out_refs, (held, owner_ref, slot_ref, sems) = refs[:-4], refs[-4:]
    count, part = held.shape
    layer = lax.axis_index("layer")
    start = pl.multiple_of(layer * part, part)
    *small, copy = start_copies(
        [
            (owner_hbm, owner_ref),
            (slot_hbm, slot_ref),
            (tasks_ref.at[:, pl.ds(start, part)], held),
        ],
        sems,
    )
    for each in small:
        each.wait()
    block_rows, block_cols = block_shape
    slot_row = slot_ref[...]
    slot_row = lax.rem(slot_row, block_cols) * block_rows + lax.div(slot_row, block_cols)
    across = lax.broadcasted_iota(jnp.int32, (count, count), 1)
    down = lax.broadcasted_iota(jnp.int32, (count, count), 0)
    slot_col = jnp.sum(
        jnp.where(across == down, slot_row.astype(jnp.float32), 0.0), axis=1, keepdims=True
    )
    owner_row = owner_ref[...]
    if paired:
        owner_row = owner_row ^ (
            lax.axis_index("row") * lax.axis_size("col") + lax.axis_index("col")
        )
    same = (lax.broadcasted_iota(jnp.int32, (owners, count), 0) == owner_row).astype(jnp.float32)
    before = (down < across).astype(jnp.float32).astype(jnp.bfloat16)
    ahead = jnp.dot(same.astype(jnp.bfloat16), before, preferred_element_type=jnp.float32)
    placed = jnp.sum(ahead * same, axis=0, keepdims=True).astype(jnp.int32)
    target = owner_row * capacity + placed
    places = owners * capacity
    move = (
        (lax.broadcasted_iota(jnp.int32, (places, count), 0) == target)
        .astype(jnp.float32)
        .astype(jnp.bfloat16)
    )

    def put(at, end, blocks):
        moved = jnp.dot(move, blocks, preferred_element_type=jnp.float32).astype(jnp.bfloat16)
        if not paired:
            out_refs[0][:, at:end] = moved
            return
        n_row, n_col = lax.axis_size("row"), lax.axis_size("col")
        if at < part // 2 + LANES:
            each = n_col * capacity
            for down, out_ref in enumerate(out_refs[:n_row]):
                out_ref[:, at:end] = moved[down * each : (down + 1) * each]
            return
        at, end = at - (part // 2 + LANES), end - (part // 2 + LANES)
        for over, out_ref in enumerate(out_refs[n_row:]):
            for down in range(n_row):
                place = (down * n_col + over) * capacity
                out_ref[down * capacity : (down + 1) * capacity, at:end] = moved[
                    place : place + capacity
                ]

    slots = jnp.broadcast_to(slot_col, (count, LANES)).astype(jnp.bfloat16)
    put(0, LANES, slots)
    copy.wait()
    step = 512
    for at in range(0, part, step):
        put(LANES + at, LANES + at + step, held[:, at : at + step])


def mix_kernel(arrivals, capacity, *refs):
    for shift, out_ref in enumerate(refs[arrivals:], 1):
        for index, ref in enumerate(refs[:arrivals][::-1]):
            out_ref[index * capacity : (index + 1) * capacity, :] = ref[
                shift * capacity : (shift + 1) * capacity, :
            ]


def token_kernel(*refs):
    refs[-1][...] = jnp.zeros_like(refs[-1])


def build_kernel(half, paired, occ_ref, marks_ref, *refs):
    out_ref, sorted_ref, tall = refs[-3:]
    layers = lax.axis_size("layer")
    block_rows, cols = out_ref.shape[0], out_ref.shape[2]
    part_rows = BLK // layers // 2
    block_cols = cols // BLK
    rows = block_rows * part_rows
    part = part_rows * BLK
    front = 0
    if half:
        got_refs, before = refs[1 if paired else 0 : -5][::-1], refs[-5:-3]
        for ref, old_ref in zip((out_ref, sorted_ref), before):
            ref[:, :part_rows] = old_ref[...]
    else:
        got_refs, held_ref = refs[:-4][::-1], refs[-4]
        front = LANES

    def got(at, end):
        if not paired:
            skip = half * (LANES + part)
            return got_refs[0][:, skip + at : skip + end]
        n_row, n_col = lax.axis_size("row"), lax.axis_size("col")
        if half:
            capacity = got_refs[0].shape[0] // n_row
            parts = [ref[:capacity, at:end] for ref in got_refs[:n_col]]
            parts += [ref[:, at:end] for ref in got_refs[n_col:]]
        else:
            capacity = got_refs[0].shape[0] // n_col
            parts = []
            for down in range(n_row):
                place = slice(down * capacity, (down + 1) * capacity)
                parts.append(got_refs[down][:capacity, at:end])
                parts += [ref[place, at:end] for ref in got_refs[n_row:]]
        return jnp.concatenate(parts, axis=0)

    if half:
        marks = marks_ref[...]
    else:
        slots = got(0, LANES).astype(jnp.float32)
        lane = lax.broadcasted_iota(jnp.int32, slots.shape, 1).astype(jnp.float32)
        which = lax.broadcasted_iota(jnp.int32, (block_cols, LANES), 1)
        spread = lax.div(which, block_rows) == lax.broadcasted_iota(jnp.int32, which.shape, 0)
        which = lax.broadcasted_iota(jnp.int32, (block_rows, LANES), 1)
        here = lax.rem(which, block_rows) == lax.broadcasted_iota(jnp.int32, which.shape, 0)
        pattern = jnp.dot(
            marks_ref[...].astype(jnp.float32),
            spread.astype(jnp.float32),
            preferred_element_type=jnp.float32,
        )
        pattern = jnp.sum(jnp.where(here, pattern, 0.0), axis=0, keepdims=True)
        marks = jnp.where(slots == lane, pattern, 0.0)
        marks = marks.T[: block_rows * block_cols].astype(jnp.bfloat16)
        held_ref[...] = marks
    low = lax.broadcasted_iota(jnp.int32, (block_rows, LANES), 1) < BLK
    step = 256
    for at in range(0, part, step):
        summed = jnp.dot(
            marks, got(front + at, front + at + step), preferred_element_type=jnp.float32
        )
        for pair in range(step // LANES):
            lanes = slice(pair * LANES, (pair + 1) * LANES)
            row = (at // LANES + pair) * 2
            for twin in range(block_cols // 2):
                left = summed[twin * 2 * block_rows : (twin * 2 + 1) * block_rows, lanes]
                right = summed[(twin * 2 + 1) * block_rows : (twin * 2 + 2) * block_rows, lanes]
                tall[twin, pl.ds(row, block_rows, stride=part_rows), :] = jnp.where(
                    low, left, pltpu.roll(right, BLK, 1)
                )
                tall[twin, pl.ds(row + 1, block_rows, stride=part_rows), :] = jnp.where(
                    low, pltpu.roll(left, BLK, 1), right
                )
    tile_rows = block_rows * BLK
    row_here = (lax.axis_index("layer") * 2 + half) * part_rows
    row_start = lax.axis_index("row") * tile_rows + row_here
    col_start = lax.axis_index("col") * cols
    index = lax.broadcasted_iota(jnp.int32, (rows, LANES), 0)
    inside = lax.div(index, part_rows) * BLK + lax.rem(index, part_rows)
    row_id = row_start + inside
    lane = lax.broadcasted_iota(jnp.int32, (rows, LANES), 1)
    occ = jnp.zeros((rows, 1), jnp.float32)
    for at in range(0, tile_rows, LANES):
        mine = jnp.where(row_here + inside == at + lane, occ_ref[:, at : at + LANES], 0.0)
        occ = occ + jnp.sum(mine, axis=1, keepdims=True)
    values = []
    for twin in range(block_cols // 2):
        diagonal = jnp.where(row_id == col_start + twin * LANES + lane, occ, 0.0)
        values.append(tall[twin] + diagonal)
    here = slice(half * part_rows, (half + 1) * part_rows)

    def put(ref, at, value):
        ref[:, here, at : at + LANES] = value.astype(jnp.bfloat16).reshape(
            block_rows, part_rows, LANES
        )

    for twin, value in enumerate(values):
        put(out_ref, twin * LANES, value)
    quarter = LANES // 4
    spot = lax.div(lane, quarter)
    for twin in range(0, block_cols // 2, 2):
        first, second = values[twin], values[twin + 1]
        at = twin // (block_rows // 2) * tile_rows + twin % (block_rows // 2) // 2 * LANES
        back, ahead = pltpu.roll(first, 3 * quarter, 1), pltpu.roll(second, quarter, 1)
        far_back, far_ahead = pltpu.roll(first, 2 * quarter, 1), pltpu.roll(second, 2 * quarter, 1)
        put(
            sorted_ref,
            at,
            jnp.where(
                spot == 0, first, jnp.where(spot == 1, back, jnp.where(spot == 2, far_ahead, ahead))
            ),
        )
        put(
            sorted_ref,
            at + tile_rows // 2,
            jnp.where(
                spot == 0, back, jnp.where(spot == 1, far_back, jnp.where(spot == 2, ahead, second))
            ),
        )


def start_copies(pairs, sems):
    copies = [
        pltpu.make_async_copy(source, target, sems.at[index])
        for index, (source, target) in enumerate(pairs)
    ]
    for copy in copies:
        copy.start()
    return copies


def split(values, sizes):
    ends = [sum(sizes[: index + 1]) for index in range(len(sizes))]
    return [values[end - size : end] for end, size in zip(ends, sizes)]


def joined(parts):
    return flat(jnp.concatenate([part[...] for part in parts], axis=0))


def left_blocks(tile_rows, cols):
    width = tile_rows // 2
    return [
        (at // tile_rows, at % tile_rows // width, slice(at, at + width))
        for at in range(0, cols, width)
    ]


def flat(value):
    return value.reshape(-1, value.shape[-1])


def near_square_kernel(n_col, n_row, *refs):
    lefts, pieces = refs[: n_col - 1], refs[n_col - 1 : n_col - 1 + n_row]
    sum_ref, other_ref, met_ref, give_ref, left, sems = refs[n_col - 1 + n_row :]
    row, col, layer = (lax.axis_index(axis) for axis in ("row", "col", "layer"))
    cols = sum_ref.shape[1]
    per_col = n_row // n_col
    pairs = [
        (piece.at[:, :, lanes], left.at[(col ^ shift) * per_col + block, which])
        for shift, piece in enumerate(lefts)
        for block, which, lanes in left_blocks(cols // per_col, cols)
    ]
    inner = len(pairs)
    here = give_ref.shape[1]
    pairs += [
        (piece.at[pl.ds((1 - layer) * here, here)], give_ref.at[col ^ shift])
        for shift, piece in enumerate(lefts)
    ]
    copies = start_copies(pairs, sems)
    last = col ^ (n_col - 1)
    for block in range(per_col):
        left[last * per_col + block] = jnp.zeros(left.shape[1:], left.dtype)
    for shift in range(n_row):

        @pl.when(lax.div(row ^ shift, per_col) == last)
        def _(shift=shift):
            met_ref[lax.rem(row ^ shift, per_col)] = flat(pieces[shift][...])

    for copy in copies[:inner]:
        copy.wait()
    total = jnp.zeros(sum_ref.shape, jnp.float32)
    for shift in range(n_row):
        total = total + jnp.dot(
            flat(left[row ^ shift, layer]),
            flat(pieces[shift][...]),
            preferred_element_type=jnp.float32,
        )
        other_ref[shift] = flat(left[row ^ shift, 1 - layer])
    sum_ref[...] = total
    for copy in copies[inner:]:
        copy.wait()


def far_square_kernel(n_col, n_row, *refs):
    sum_ref, other_ref, met_ref = refs[:3]
    mates, left_ref = refs[3 : 3 + n_row], refs[3 + n_row]
    low_ref, give_ref, sem = refs[5 + n_row :]
    row, col, layer = (lax.axis_index(axis) for axis in ("row", "col", "layer"))
    here = give_ref.shape[1]
    copy = pltpu.make_async_copy(
        left_ref.at[pl.ds((1 - layer) * here, here)], give_ref.at[col ^ (n_col - 1)], sem
    )
    copy.start()
    per_col = met_ref.shape[0]
    width = other_ref.shape[2]

    def columns(block, which):
        start = pl.multiple_of((block * 2 + which) * width, width)
        return flat(left_ref[:, :, pl.ds(start, width)])

    total = sum_ref[...]
    for block in range(per_col):
        total = total + jnp.dot(
            columns(block, layer), met_ref[block], preferred_element_type=jnp.float32
        )
    for shift, mate in enumerate(mates):
        met = row ^ shift
        left = jnp.where(
            lax.div(met, per_col) == col ^ (n_col - 1),
            columns(lax.rem(met, per_col), 1 - layer),
            other_ref[shift],
        )
        total = total + jnp.dot(left, flat(mate[...]), preferred_element_type=jnp.float32)
    low_ref[...] = total.astype(jnp.bfloat16).reshape(low_ref.shape)
    copy.wait()


def near_cube_kernel(n_col, sizes, *refs):
    lefts, given, pattern_ref = refs[:n_col], refs[n_col], refs[n_col + 1]
    n_row, count = len(sizes), n_col + 2 + sum(sizes)
    pieces, mates = split(refs[n_col + 2 : count], sizes), refs[count : count + n_row - 1]
    sum_ref, mask_ref, other_ref, left, own, sems = refs[count + n_row - 1 :]
    row, col, layer = (lax.axis_index(axis) for axis in ("row", "col", "layer"))
    rows, cols = sum_ref.shape
    per_col = n_row // n_col
    here = given.shape[1]
    mine = pl.ds(layer * here, here)
    pairs = []
    for block, which, lanes in left_blocks(cols // per_col, cols):
        for shift, piece in enumerate(lefts):
            at = (col ^ shift) * per_col + block
            pairs.append((piece.at[mine, :, lanes], left.at[at, which, :, layer]))
            pairs.append(
                (given.at[col ^ shift, :, :, lanes], left.at[at, which, :, 1 - layer])
            )
    copies = start_copies(pairs, sems)
    own[:, layer] = pieces[0][0][mine]
    own[:, 1 - layer] = mates[0][mine]
    pattern = pattern_ref[...].astype(jnp.float32).astype(jnp.bfloat16)
    block_rows, block_cols = pattern.shape
    across = lax.broadcasted_iota(jnp.int32, (block_cols, cols), 1)
    which = lax.broadcasted_iota(jnp.int32, (block_cols, cols), 0)
    wide = (lax.div(across, BLK) == which).astype(jnp.float32).astype(jnp.bfloat16)
    down = lax.broadcasted_iota(jnp.int32, (rows, block_rows), 0) + layer * rows
    which = lax.broadcasted_iota(jnp.int32, (rows, block_rows), 1)
    tall = (lax.div(down, BLK) == which).astype(jnp.float32).astype(jnp.bfloat16)
    tall = jnp.dot(tall, pattern, preferred_element_type=jnp.float32).astype(jnp.bfloat16)
    mask = jnp.dot(tall, wide, preferred_element_type=jnp.float32)
    mask_ref[...] = mask.astype(jnp.bfloat16)
    total = 1.5 * flat(own[...]).astype(jnp.float32)
    for copy in copies:
        copy.wait()
    for shift in range(n_row):
        total = total - jnp.dot(
            flat(left[row ^ shift, layer]),
            joined(pieces[shift]),
            preferred_element_type=jnp.float32,
        )
    for shift, mate in enumerate(mates):
        total = total - jnp.dot(
            flat(left[row ^ shift, 1 - layer]),
            flat(mate[...]),
            preferred_element_type=jnp.float32,
        )
    other_ref[...] = flat(left[row ^ (n_row - 1), 1 - layer])
    sum_ref[...] = total


def far_cube_kernel(sum_ref, mask_ref, left_ref, *refs):
    mates, out_ref = refs[:-2], refs[-1]
    total = sum_ref[...] - jnp.dot(
        left_ref[...], joined(mates), preferred_element_type=jnp.float32
    )
    out_ref[...] = mask_ref[...].astype(jnp.float32) * (2.0 * total)


def xor_pairs(axis, shift):
    return [(i, i ^ shift) for i in range(lax.axis_size(axis))]


def gather(piece, axis):
    return [piece] + [
        lax.ppermute(piece, axis, xor_pairs(axis, shift))
        for shift in range(1, lax.axis_size(axis))
    ]


def exchange(first, second, capacity):
    def relay(parcels, out_axis, in_axis, weight):
        arrived = [parcels[0]] + [
            lax.ppermute(parcel, out_axis, xor_pairs(out_axis, shift))
            for shift, parcel in enumerate(parcels)
            if shift
        ]
        steps = lax.axis_size(in_axis)
        shape = (len(arrived) * capacity, parcels[0].shape[1])
        mixed = pl.pallas_call(
            functools.partial(mix_kernel, len(arrived), capacity),
            out_shape=[jax.ShapeDtypeStruct(shape, jnp.bfloat16)] * (steps - 1),
            in_specs=[whole_ref()] * len(arrived),
            out_specs=[whole_ref()] * (steps - 1),
            compiler_params=params(4 * steps * shape[0] * shape[1]),
            cost_estimate=cost(weight, 4 * steps * shape[0] * shape[1]),
            name="mix",
        )(*arrived[::-1])
        return arrived + [
            lax.ppermute(parcel, in_axis, xor_pairs(in_axis, shift))
            for shift, parcel in enumerate(mixed, 1)
        ]

    first = relay(first, "row", "col", EARLY)
    second = relay(second, "col", "row", LATE)
    return first, [*second, token(second, EXTRA)]


def after(value, *earlier):
    return lax.optimization_barrier((value, earlier))[0]


def token(values, weight):
    return pl.pallas_call(
        token_kernel,
        out_shape=jax.ShapeDtypeStruct((8, LANES), jnp.float32),
        in_specs=[any_ref()] * len(values),
        out_specs=whole_ref(),
        compiler_params=params(0),
        cost_estimate=cost(weight, 0),
        name="token",
    )(*values)


def gather_line(piece):
    count = lax.axis_size("col")
    pieces = {0: piece}
    step = count // 2
    while step:
        pieces |= {
            shift + step: lax.ppermute(held, "col", xor_pairs("col", step))
            for shift, held in pieces.items()
        }
        step //= 2
    return [pieces[shift] for shift in range(count)]


def gather_square(piece):
    if lax.axis_size("row") != 4:
        return [[held] for held in gather(piece, "row")]
    one, two = (lax.ppermute(piece, "row", xor_pairs("row", shift)) for shift in (1, 2))
    middle = piece.shape[0] // 2
    far = [
        lax.ppermute(two[:middle], "row", xor_pairs("row", 1)),
        lax.ppermute(one[middle:], "row", xor_pairs("row", 2)),
    ]
    return [[piece], [one], [two], far]


def swap(piece):
    return lax.ppermute(piece, "layer", xor_pairs("layer", 1))


def on_device(tasks, task_owner, task_slot, p_pattern, c_pattern, occupations):
    n_row, n_col, layers = (lax.axis_size(axis) for axis in ("row", "col", "layer"))
    owners = n_row * n_col
    count = tasks.shape[0]
    capacity = max(2, 2 * count // owners)
    places = owners * capacity
    block_rows, block_cols = p_pattern.shape
    part_rows = BLK // layers
    part = part_rows * BLK
    rows, cols = block_rows * part_rows, block_cols * BLK
    width = part + LANES
    layer = lax.axis_index("layer")

    paired = capacity % 16 == 0
    if paired:
        parcels = [(n_col * capacity, part // 2 + LANES)] * n_row
        parcels += [(n_row * capacity, part - part // 2)] * n_col
    else:
        parcels = [(places, width)]
    sent = pl.pallas_call(
        functools.partial(pack_kernel, owners, capacity, p_pattern.shape, paired),
        out_shape=[jax.ShapeDtypeStruct(shape, jnp.bfloat16) for shape in parcels],
        in_specs=[any_ref()] * 3,
        out_specs=[whole_ref()] * len(parcels),
        scratch_shapes=[
            pltpu.VMEM((count, part), jnp.bfloat16),
            pltpu.VMEM((1, count), jnp.int32),
            pltpu.VMEM((1, count), jnp.int32),
            pltpu.SemaphoreType.DMA((3,)),
        ],
        compiler_params=pltpu.CompilerParams(vmem_limit_bytes=PACK_VMEM),
        cost_estimate=cost(2 * places * count * width, 2 * (places + count) * width),
        name="pack",
    )(tasks, task_owner.reshape(1, count), task_slot.reshape(1, count))
    if paired:
        got = list(exchange(sent[:n_row], sent[n_row:], capacity))
    else:
        got = [
            [
                lax.all_to_all(
                    sent[0].reshape(owners, capacity, width),
                    ("row", "col"),
                    split_axis=0,
                    concat_axis=0,
                    tiled=True,
                ).reshape(places, width)
            ]
        ] * 2

    slots_here = block_rows * block_cols
    half_shape = jax.ShapeDtypeStruct((block_rows, part_rows // 2, cols), jnp.bfloat16)
    piece_shape = jax.ShapeDtypeStruct((block_rows, part_rows, cols), jnp.bfloat16)
    marks_shape = jax.ShapeDtypeStruct((slots_here, places), jnp.bfloat16)

    def build(half, marks, *blocks):
        return pl.pallas_call(
            functools.partial(build_kernel, half, paired),
            out_shape=[piece_shape] * 2 if half else [marks_shape, half_shape, half_shape],
            in_specs=[whole_ref()] * (2 + len(blocks)),
            out_specs=[whole_ref()] * (2 if half else 3),
            scratch_shapes=[pltpu.VMEM((cols // LANES, rows // 2, LANES), jnp.float32)],
            compiler_params=params(2 * places * width + 8 * rows * cols),
            cost_estimate=cost(places * slots_here * part, places * width),
            name="build",
        )(occupations.reshape(1, block_rows * BLK), marks, *blocks)

    marks, *first_half = build(0, p_pattern, *got[0][::-1])
    density, ordered = build(1, marks, *got[1][::-1], *first_half)

    lefts = gather_line(ordered)
    mate = swap(density)
    pieces = gather(after(density, mate), "row")
    pieces[0] = density
    ahead = (lefts[1], lefts[n_col // 2])
    mates = [mate] + [swap(after(piece, *ahead)) for piece in pieces[1:]]
    flops = 2 * rows * cols * n_col * cols
    half_width = block_rows * BLK // layers
    panel_bytes = 2 * n_row * layers * rows * half_width
    sum_shape = jax.ShapeDtypeStruct((rows, cols), jnp.float32)
    other_shape = jax.ShapeDtypeStruct((n_row, rows, half_width), jnp.bfloat16)
    met_shape = jax.ShapeDtypeStruct((n_row // n_col, rows, cols), jnp.bfloat16)
    here = block_rows // layers
    give_shape = jax.ShapeDtypeStruct((n_col, here, part_rows, cols), jnp.bfloat16)
    partial, other, met, give = pl.pallas_call(
        functools.partial(near_square_kernel, n_col, n_row),
        out_shape=[sum_shape, other_shape, met_shape, give_shape],
        in_specs=[any_ref()] * (n_col - 1) + [whole_ref()] * n_row,
        out_specs=[whole_ref()] * 3 + [any_ref()],
        scratch_shapes=[
            pltpu.VMEM((n_row, layers, block_rows, part_rows, half_width), jnp.bfloat16),
            pltpu.SemaphoreType.DMA((n_row * layers + n_col,)),
        ],
        compiler_params=params(2 * panel_bytes + 16 * rows * cols),
        cost_estimate=cost(0, 0),
        name="near_square",
    )(*lefts[:-1], *pieces)
    square, give = pl.pallas_call(
        functools.partial(far_square_kernel, n_col, n_row),
        out_shape=[piece_shape, give_shape],
        in_specs=[whole_ref()] * (4 + n_row) + [any_ref()],
        out_specs=[whole_ref(), any_ref()],
        scratch_shapes=[pltpu.SemaphoreType.DMA],
        input_output_aliases={4 + n_row: 1},
        compiler_params=params(panel_bytes + 16 * rows * cols),
        cost_estimate=cost(0, 0),
        name="far_square",
    )(partial, other, met, *mates, lefts[-1], give)

    pieces = gather_square(square)
    mates = [[swap(part) for part in parts] for parts in pieces]
    if len(pieces[-1]) > 1:
        mates[1:3] = [[swap(after(pieces[shift][0], pieces[3 - shift][0]))] for shift in (1, 2)]
    received = swap(after(give, pieces[1][0], pieces[2][0]))
    sizes = [len(parts) for parts in pieces]
    pieces, mates = ([part for parts in held for part in parts] for held in (pieces, mates))
    partial, mask, other = pl.pallas_call(
        functools.partial(near_cube_kernel, n_col, sizes),
        out_shape=[
            sum_shape,
            jax.ShapeDtypeStruct((rows, cols), jnp.bfloat16),
            jax.ShapeDtypeStruct((rows, half_width), jnp.bfloat16),
        ],
        in_specs=[any_ref()] * (n_col + 1) + [whole_ref()] * (n_row + len(pieces)),
        out_specs=[whole_ref()] * 3,
        scratch_shapes=[
            pltpu.VMEM((n_row, layers, here, layers, part_rows, half_width), jnp.bfloat16),
            pltpu.VMEM((here, layers, part_rows, cols), jnp.bfloat16),
            pltpu.SemaphoreType.DMA((2 * n_row * layers,)),
        ],
        compiler_params=params(2 * panel_bytes + 16 * rows * cols),
        cost_estimate=cost(0, 0),
        name="near_cube",
    )(*lefts, received, c_pattern, *pieces, *mates[: n_row - 1])
    return pl.pallas_call(
        far_cube_kernel,
        out_shape=sum_shape,
        in_specs=[whole_ref()] * (3 + sizes[-1]) + [any_ref()],
        out_specs=whole_ref(),
        compiler_params=params(16 * rows * cols),
        cost_estimate=cost(flops // 2, 4 * 1024 * 1024),
        name="far_cube",
    )(partial, mask, other, *mates[n_row - 1 :], token(pieces[n_row - 1 :], HEAVY))


def solution(mesh):
    return jax.shard_map(
        on_device,
        mesh=mesh,
        in_specs=(
            P(("row", "col"), None),
            P(("row", "col"), None),
            P(("row", "col")),
            P("row", "col"),
            P("row", "col"),
            P("row"),
        ),
        out_specs=P(("row", "layer"), "col"),
        check_vma=False,
    )
```

profile of v0, /device:TPU:0, one launch (start us, length us, event | category | flops | bytes accessed | tf_op | source)
XLA Modules:
  0.0 74.9 jit_solution(2461670077402927833)
XLA Ops:
  0.0 0.7 copy-done.3
  0.7 1.5 %pack.1 = (bf16[64,1152]{1,0:T(8,128)(2,1)S(1)}, bf16[64,1152]{1,0:T(8,128)(2,1)S(1)}, bf16[64,1152]{1,0:T(8,128)(2,1)S(1)}, bf16[64,1152]{1,0:T(8,128)(2,1)S(1)...) custom-call(bf16[128,4096]{1,0:T(8,128)(2,1)} %tasks_ref.1, ...), custom_call_target="tpu_custom_call" | custom-call | flops 142606336 | bytes 1671168 | tf_op jit(solution)/shard_map/pack/pallas_call | solution.py:502
  2.2 3.1 %collective-permute-start.6 = (bf16[64,1024]{1,0:T(8,128)(2,1)S(1)}, bf16[64,1024]{1,0:T(8,128)(2,1)S(1)}, u32[]{:S(2)}, u32[]{:S(2)}) collective-permute-start(bf16[64,1024]{1,0:T(8,128)(2,1)S(1)} %get-tuple-element.49), channel_id=1, source_target_pairs={{0,2},{2,0},{4,6},{6,4},{1,3},{3,1},{5,7},{7,5},{8,10},{10,8},{12,... | collective-permute-start | bytes 393224 | tf_op jit(solution)/shard_map/ppermute | solution.py:413
  5.3 2.6 %collective-permute-start.7 = (bf16[64,1024]{1,0:T(8,128)(2,1)S(1)}, bf16[64,1024]{1,0:T(8,128)(2,1)S(1)}, u32[]{:S(2)}, u32[]{:S(2)}) collective-permute-start(bf16[64,1024]{1,0:T(8,128)(2,1)S(1)} %get-tuple-element.50), channel_id=1, source_target_pairs={{0,4},{2,6},{4,0},{6,2},{1,5},{3,7},{5,1},{7,3},{8,12},{10,14},{12... | collective-permute-start | bytes 393224 | tf_op jit(solution)/shard_map/ppermute | solution.py:413
  7.9 2.7 %collective-permute-start = (bf16[64,1152]{1,0:T(8,128)(2,1)S(1)}, bf16[64,1152]{1,0:T(8,128)(2,1)S(1)}, u32[]{:S(2)}, u32[]{:S(2)}) collective-permute-start(bf16[64,1152]{1,0:T(8,128)(2,1)S(1)} %get-tuple-element.40), channel_id=1, source_target_pairs={{0,24},{8,16},{16,8},{24,0},{1,25},{9,17},{17,9},{25,1},{2,26},{10... | collective-permute-start | bytes 442376 | tf_op jit(solution)/shard_map/ppermute | solution.py:413
  11.0 1.0 %collective-permute-start.2 = (bf16[64,1152]{1,0:T(8,128)(2,1)S(1)}, bf16[64,1152]{1,0:T(8,128)(2,1)S(1)}, u32[]{:S(2)}, u32[]{:S(2)}) collective-permute-start(bf16[64,1152]{1,0:T(8,128)(2,1)S(1)} %get-tuple-element.42), channel_id=1, source_target_pairs={{0,8},{8,0},{16,24},{24,16},{1,9},{9,1},{17,25},{25,17},{2,10},{10... | collective-permute-start | bytes 442376 | tf_op jit(solution)/shard_map/ppermute | solution.py:413
  12.0 6.2 %collective-permute-done.7.refs_1_.refs_2_.refs_5_ = bf16[64,1024]{1,0:T(8,128)(2,1)S(1)} collective-permute-done((bf16[64,1024]{1,0:T(8,128)(2,1)S(1)}, bf16[64,1024]{1,0:T(8,128)(2,1)S(1)}, u32[]{:S(2)}, u32[]{:S(2)}) %collective-permute-start.7) | collective-permute-done | bytes 131104 | tf_op jit(solution)/shard_map/ppermute | solution.py:413
  18.2 1.6 %collective-permute-start.10 = (bf16[64,1024]{1,0:T(8,128)(2,1)S(1)}, bf16[64,1024]{1,0:T(8,128)(2,1)S(1)}, u32[]{:S(2)}, u32[]{:S(2)}) collective-permute-start(bf16[64,1024]{1,0:T(8,128)(2,1)S(1)} %get-tuple-element.53), channel_id=1, source_target_pairs={{0,16},{8,24},{16,0},{24,8},{1,17},{9,25},{17,1},{25,9},{2,18},{10... | collective-permute-start | bytes 393224 | tf_op jit(solution)/shard_map/ppermute | solution.py:429
  19.9 2.4 %collective-permute-start.3 = (bf16[64,1152]{1,0:T(8,128)(2,1)S(1)}, bf16[64,1152]{1,0:T(8,128)(2,1)S(1)}, u32[]{:S(2)}, u32[]{:S(2)}) collective-permute-start(bf16[64,1152]{1,0:T(8,128)(2,1)S(1)} %get-tuple-element.44), channel_id=1, source_target_pairs={{0,6},{2,4},{4,2},{6,0},{1,7},{3,5},{5,3},{7,1},{8,14},{10,12},{12... | collective-permute-start | bytes 442376 | tf_op jit(solution)/shard_map/ppermute | solution.py:429
  22.2 1.1 %collective-permute-start.4 = (bf16[64,1152]{1,0:T(8,128)(2,1)S(1)}, bf16[64,1152]{1,0:T(8,128)(2,1)S(1)}, u32[]{:S(2)}, u32[]{:S(2)}) collective-permute-start(bf16[64,1152]{1,0:T(8,128)(2,1)S(1)} %get-tuple-element.45), channel_id=1, source_target_pairs={{0,4},{2,6},{4,0},{6,2},{1,5},{3,7},{5,1},{7,3},{8,12},{10,14},{12... | collective-permute-start | bytes 442376 | tf_op jit(solution)/shard_map/ppermute | solution.py:429
  23.4 1.0 %collective-permute-start.5 = (bf16[64,1152]{1,0:T(8,128)(2,1)S(1)}, bf16[64,1152]{1,0:T(8,128)(2,1)S(1)}, u32[]{:S(2)}, u32[]{:S(2)}) collective-permute-start(bf16[64,1152]{1,0:T(8,128)(2,1)S(1)} %get-tuple-element.46), channel_id=1, source_target_pairs={{0,2},{2,0},{4,6},{6,4},{1,3},{3,1},{5,7},{7,5},{8,10},{10,8},{12,... | collective-permute-start | bytes 442376 | tf_op jit(solution)/shard_map/ppermute | solution.py:429
  24.3 1.4 %collective-permute-start.11 = (bf16[64,1024]{1,0:T(8,128)(2,1)S(1)}, bf16[64,1024]{1,0:T(8,128)(2,1)S(1)}, u32[]{:S(2)}, u32[]{:S(2)}) collective-permute-start(bf16[64,1024]{1,0:T(8,128)(2,1)S(1)} %get-tuple-element.54), channel_id=1, source_target_pairs={{0,24},{8,16},{16,8},{24,0},{1,25},{9,17},{17,9},{25,1},{2,26},{10... | collective-permute-start | bytes 393224 | tf_op jit(solution)/shard_map/ppermute | solution.py:429
  26.3 3.9 %collective-permute-done.11.refs_6_.refs_1_ = bf16[64,1024]{1,0:T(8,128)(2,1)S(1)} collective-permute-done((bf16[64,1024]{1,0:T(8,128)(2,1)S(1)}, bf16[64,1024]{1,0:T(8,128)(2,1)S(1)}, u32[]{:S(2)}, u32[]{:S(2)}) %collective-permute-start.11) | collective-permute-done | bytes 131104 | tf_op jit(solution)/shard_map/ppermute | solution.py:429
  30.7 3.3 %collective-permute-done.4.refs_1_ = bf16[64,1152]{1,0:T(8,128)(2,1)S(1)} collective-permute-done((bf16[64,1152]{1,0:T(8,128)(2,1)S(1)}, bf16[64,1152]{1,0:T(8,128)(2,1)S(1)}, u32[]{:S(2)}, u32[]{:S(2)}) %collective-permute-start.4) | collective-permute-done | bytes 147488 | tf_op jit(solution)/shard_map/ppermute | solution.py:429
  34.1 0.6 build.2
  35.4 3.2 %collective-permute-start.13 = (bf16[8,32,512]{2,1,0:T(8,128)(2,1)S(1)}, bf16[8,32,512]{2,1,0:T(8,128)(2,1)S(1)}, u32[]{:S(2)}, u32[]{:S(2)}) collective-permute-start(bf16[8,32,512]{2,1,0:T(8,128)(2,1)S(1)} %get-tuple-element.57.refs_0_), channel_id=1, source_target_pairs={{0,4},{2,6},{4,0},{6,2},{1,5},{3,7},{5,1},{7,3},{8,12},{10,14},{12... | collective-permute-start | bytes 786440 | tf_op jit(solution)/shard_map/ppermute | solution.py:460
  38.6 1.7 %collective-permute-start.18 = (bf16[8,32,512]{2,1,0:T(8,128)(2,1)S(1)}, bf16[8,32,512]{2,1,0:T(8,128)(2,1)S(1)}, u32[]{:S(2)}, u32[]{:S(2)}) collective-permute-start(bf16[8,32,512]{2,1,0:T(8,128)(2,1)S(1)} %get-tuple-element.59.refs_3_), channel_id=1, source_target_pairs={{0,24},{8,16},{16,8},{24,0},{1,25},{9,17},{17,9},{25,1},{2,26},{10... | collective-permute-start | bytes 786440 | tf_op jit(solution)/shard_map/ppermute | solution.py:405
  40.3 1.7 %collective-permute-start.17 = (bf16[8,32,512]{2,1,0:T(8,128)(2,1)S(1)}, bf16[8,32,512]{2,1,0:T(8,128)(2,1)S(1)}, u32[]{:S(2)}, u32[]{:S(2)}) collective-permute-start(bf16[8,32,512]{2,1,0:T(8,128)(2,1)S(1)} %get-tuple-element.59.refs_3_), channel_id=1, source_target_pairs={{0,16},{8,24},{16,0},{24,8},{1,17},{9,25},{17,1},{25,9},{2,18},{10... | collective-permute-start | bytes 786440 | tf_op jit(solution)/shard_map/ppermute | solution.py:405
  42.1 8.8 %collective-permute-done.13.refs_2_ = bf16[8,32,512]{2,1,0:T(8,128)(2,1)S(1)} collective-permute-done((bf16[8,32,512]{2,1,0:T(8,128)(2,1)S(1)}, bf16[8,32,512]{2,1,0:T(8,128)(2,1)S(1)}, u32[]{:S(2)}, u32[]{:S(2)}) %collective-permute-start.13) | collective-permute-done | bytes 262176 | tf_op jit(solution)/shard_map/ppermute | solution.py:460
  51.2 2.0 %collective-permute-done.17.refs_5_ = bf16[8,32,512]{2,1,0:T(8,128)(2,1)S(1)} collective-permute-done((bf16[8,32,512]{2,1,0:T(8,128)(2,1)S(1)}, bf16[8,32,512]{2,1,0:T(8,128)(2,1)S(1)}, u32[]{:S(2)}, u32[]{:S(2)}) %collective-permute-start.17) | collective-permute-done | bytes 262176 | tf_op jit(solution)/shard_map/ppermute | solution.py:405
  53.7 1.2 %near_square.1 = (f32[256,512]{1,0:T(8,128)S(1)}, bf16[4,256,256]{2,1,0:T(8,128)(2,1)S(1)}, bf16[1,256,512]{2,1,0:T(8,128)(2,1)S(1)}, bf16[4,4,32,512]{3,2,1,0:T(8,128)(2,1)S(1)}) custom-call(bf16[8,32,512]{2,1,0:T(8,128)(2,1)S(1)} %get-tuple-element.57.refs_0_, bf16[8,32,512]{2,1,0:T(8,128)(2,1)S(1)} %collective-permute-done.12.refs_1_, ...), custom_call_target="tpu_custom_call" | custom-call | tf_op jit(solution)/shard_map/near_square/pallas_call | solution.py:566
  54.9 2.6 %collective-permute-done.14.refs_7_.refs_3_ = bf16[8,32,512]{2,1,0:T(8,128)(2,1)S(1)} collective-permute-done((bf16[8,32,512]{2,1,0:T(8,128)(2,1)S(1)}, bf16[8,32,512]{2,1,0:T(8,128)(2,1)S(1)}, u32[]{:S(2)}, u32[]{:S(2)}) %collective-permute-start.14) | collective-permute-done | bytes 262176 | tf_op jit(solution)/shard_map/ppermute | solution.py:460
  57.5 0.7 far_square.1
  58.2 1.5 %collective-permute-start.23 = (bf16[8,32,512]{2,1,0:T(8,128)(2,1)S(1)}, bf16[8,32,512]{2,1,0:T(8,128)(2,1)S(1)}, u32[]{:S(2)}, u32[]{:S(2)}) collective-permute-start(bf16[8,32,512]{2,1,0:T(8,128)(2,1)S(1)} %get-tuple-element.68.refs_6_), channel_id=1, source_target_pairs={{0,16},{8,24},{16,0},{24,8},{1,17},{9,25},{17,1},{25,9},{2,18},{10... | collective-permute-start | bytes 786440 | tf_op jit(solution)/shard_map/ppermute | solution.py:470
  59.7 0.9 %collective-permute-start.22 = (bf16[8,32,512]{2,1,0:T(8,128)(2,1)S(1)}, bf16[8,32,512]{2,1,0:T(8,128)(2,1)S(1)}, u32[]{:S(2)}, u32[]{:S(2)}) collective-permute-start(bf16[8,32,512]{2,1,0:T(8,128)(2,1)S(1)} %get-tuple-element.68.refs_6_), channel_id=1, source_target_pairs={{0,8},{8,0},{16,24},{24,16},{1,9},{9,1},{17,25},{25,17},{2,10},{10... | collective-permute-start | bytes 786440 | tf_op jit(solution)/shard_map/ppermute | solution.py:470
  60.5 4.1 %collective-permute-done.23.refs_8_ = bf16[8,32,512]{2,1,0:T(8,128)(2,1)S(1)} collective-permute-done((bf16[8,32,512]{2,1,0:T(8,128)(2,1)S(1)}, bf16[8,32,512]{2,1,0:T(8,128)(2,1)S(1)}, u32[]{:S(2)}, u32[]{:S(2)}) %collective-permute-start.23) | collective-permute-done | bytes 262176 | tf_op jit(solution)/shard_map/ppermute | solution.py:470
  64.7 2.0 %collective-permute-start.25 = (bf16[4,32,512]{2,1,0:T(8,128)(2,1)S(1)}, bf16[4,32,512]{2,1,0:T(8,128)(2,1)S(1)}, u32[]{:S(2)}, u32[]{:S(2)}) collective-permute-start(bf16[4,32,512]{2,1,0:T(8,128)(2,1)S(1)} %slice.8), channel_id=1, source_target_pairs={{0,8},{8,0},{16,24},{24,16},{1,9},{9,1},{17,25},{25,17},{2,10},{10... | collective-permute-start | bytes 393224 | tf_op jit(solution)/shard_map/ppermute | solution.py:473
  66.7 0.8 %collective-permute-done.22.refs_7_ = bf16[8,32,512]{2,1,0:T(8,128)(2,1)S(1)} collective-permute-done((bf16[8,32,512]{2,1,0:T(8,128)(2,1)S(1)}, bf16[8,32,512]{2,1,0:T(8,128)(2,1)S(1)}, u32[]{:S(2)}, u32[]{:S(2)}) %collective-permute-start.22) | collective-permute-done | bytes 262176 | tf_op jit(solution)/shard_map/ppermute | solution.py:470
  68.2 1.5 %collective-permute-done.25.refs_9_.refs_0_ = bf16[4,32,512]{2,1,0:T(8,128)(2,1)S(1)} collective-permute-done((bf16[4,32,512]{2,1,0:T(8,128)(2,1)S(1)}, bf16[4,32,512]{2,1,0:T(8,128)(2,1)S(1)}, u32[]{:S(2)}, u32[]{:S(2)}) %collective-permute-start.25) | collective-permute-done | bytes 131104 | tf_op jit(solution)/shard_map/ppermute | solution.py:473
  69.7 2.8 %collective-permute-done.26.refs_10_.refs_1_ = bf16[4,32,512]{2,1,0:T(8,128)(2,1)S(1)} collective-permute-done((bf16[4,32,512]{2,1,0:T(8,128)(2,1)S(1)}, bf16[4,32,512]{2,1,0:T(8,128)(2,1)S(1)}, u32[]{:S(2)}, u32[]{:S(2)}) %collective-permute-start.26) | collective-permute-done | bytes 131104 | tf_op jit(solution)/shard_map/ppermute | solution.py:474
  72.6 1.3 %near_cube.1 = (f32[256,512]{1,0:T(8,128)S(1)}, bf16[256,512]{1,0:T(8,128)(2,1)S(1)}, bf16[256,256]{1,0:T(8,128)(2,1)S(1)}) custom-call(bf16[8,32,512]{2,1,0:T(8,128)(2,1)S(1)} %get-tuple-element.57.refs_0_, bf16[8,32,512]{2,1,0:T(8,128)(2,1)S(1)} %collective-permute-done.12.refs_1_, bf16[8,32,512]{2,1,0:T(8,128)(2,1)S(1)} %collective-permute-done.13.refs_2_, ...), custom_call_target="tpu_custom_call" | custom-call | tf_op jit(solution)/shard_map/near_cube/pallas_call | solution.py:598
  73.9 1.0 %far_cube.1 = f32[256,512]{1,0:T(8,128)} custom-call(f32[256,512]{1,0:T(8,128)S(1)} %get-tuple-element.72.sum_ref, bf16[256,512]{1,0:T(8,128)(2,1)S(1)} %get-tuple-element.73.mask_ref, bf16[256,256]{1,0:T(8,128)(2,1)S(1)} %get-tuple-element.74.left_ref, bf16[4,32,512]{2,1,0:T(8,128)(2,1)S(1)} %collective-permute-done.30.refs_0_, ...), custom_call_target="tpu_custom_call" | custom-call | flops 268435456 | bytes 4194304 | tf_op jit(solution)/shard_map/far_cube/pallas_call | solution.py:616
  (55 shorter events, 4.0 us)
Async XLA Ops:
  2.2 8.9 %collective-permute-start.6 = (bf16[64,1024]{1,0:T(8,128)(2,1)S(1)}, bf16[64,1024]{1,0:T(8,128)(2,1)S(1)}, u32[]{:S(2)}, u32[]{:S(2)}) collective-permute-start(bf16[64,1024]{1,0:T(8,128)(2,1)S(1)} %get-tuple-element.49), channel_id=1, source_target_pairs={{0,2},{2,0},{4,6},{6,4},{1,3},{3,1},{5,7},{7,5},{8,10},{10,8},{12,... | collective-permute-start | bytes 393224 | tf_op jit(solution)/shard_map/ppermute | solution.py:413
  5.3 12.9 %collective-permute-start.7 = (bf16[64,1024]{1,0:T(8,128)(2,1)S(1)}, bf16[64,1024]{1,0:T(8,128)(2,1)S(1)}, u32[]{:S(2)}, u32[]{:S(2)}) collective-permute-start(bf16[64,1024]{1,0:T(8,128)(2,1)S(1)} %get-tuple-element.50), channel_id=1, source_target_pairs={{0,4},{2,6},{4,0},{6,2},{1,5},{3,7},{5,1},{7,3},{8,12},{10,14},{12... | collective-permute-start | bytes 393224 | tf_op jit(solution)/shard_map/ppermute | solution.py:413
  7.9 10.3 %collective-permute-start.8 = (bf16[64,1024]{1,0:T(8,128)(2,1)S(1)}, bf16[64,1024]{1,0:T(8,128)(2,1)S(1)}, u32[]{:S(2)}, u32[]{:S(2)}) collective-permute-start(bf16[64,1024]{1,0:T(8,128)(2,1)S(1)} %get-tuple-element.51), channel_id=1, source_target_pairs={{0,6},{2,4},{4,2},{6,0},{1,7},{3,5},{5,3},{7,1},{8,14},{10,12},{12... | collective-permute-start | bytes 393224 | tf_op jit(solution)/shard_map/ppermute | solution.py:413
  7.9 12.0 %collective-permute-start = (bf16[64,1152]{1,0:T(8,128)(2,1)S(1)}, bf16[64,1152]{1,0:T(8,128)(2,1)S(1)}, u32[]{:S(2)}, u32[]{:S(2)}) collective-permute-start(bf16[64,1152]{1,0:T(8,128)(2,1)S(1)} %get-tuple-element.40), channel_id=1, source_target_pairs={{0,24},{8,16},{16,8},{24,0},{1,25},{9,17},{17,9},{25,1},{2,26},{10... | collective-permute-start | bytes 442376 | tf_op jit(solution)/shard_map/ppermute | solution.py:413
  10.5 9.3 %collective-permute-start.1 = (bf16[64,1152]{1,0:T(8,128)(2,1)S(1)}, bf16[64,1152]{1,0:T(8,128)(2,1)S(1)}, u32[]{:S(2)}, u32[]{:S(2)}) collective-permute-start(bf16[64,1152]{1,0:T(8,128)(2,1)S(1)} %get-tuple-element.41), channel_id=1, source_target_pairs={{0,16},{8,24},{16,0},{24,8},{1,17},{9,25},{17,1},{25,9},{2,18},{10... | collective-permute-start | bytes 442376 | tf_op jit(solution)/shard_map/ppermute | solution.py:413
  11.0 8.8 %collective-permute-start.2 = (bf16[64,1152]{1,0:T(8,128)(2,1)S(1)}, bf16[64,1152]{1,0:T(8,128)(2,1)S(1)}, u32[]{:S(2)}, u32[]{:S(2)}) collective-permute-start(bf16[64,1152]{1,0:T(8,128)(2,1)S(1)} %get-tuple-element.42), channel_id=1, source_target_pairs={{0,8},{8,0},{16,24},{24,16},{1,9},{9,1},{17,25},{25,17},{2,10},{10... | collective-permute-start | bytes 442376 | tf_op jit(solution)/shard_map/ppermute | solution.py:413
  18.2 7.5 %collective-permute-start.10 = (bf16[64,1024]{1,0:T(8,128)(2,1)S(1)}, bf16[64,1024]{1,0:T(8,128)(2,1)S(1)}, u32[]{:S(2)}, u32[]{:S(2)}) collective-permute-start(bf16[64,1024]{1,0:T(8,128)(2,1)S(1)} %get-tuple-element.53), channel_id=1, source_target_pairs={{0,16},{8,24},{16,0},{24,8},{1,17},{9,25},{17,1},{25,9},{2,18},{10... | collective-permute-start | bytes 393224 | tf_op jit(solution)/shard_map/ppermute | solution.py:429
  19.9 10.9 %collective-permute-start.3 = (bf16[64,1152]{1,0:T(8,128)(2,1)S(1)}, bf16[64,1152]{1,0:T(8,128)(2,1)S(1)}, u32[]{:S(2)}, u32[]{:S(2)}) collective-permute-start(bf16[64,1152]{1,0:T(8,128)(2,1)S(1)} %get-tuple-element.44), channel_id=1, source_target_pairs={{0,6},{2,4},{4,2},{6,0},{1,7},{3,5},{5,3},{7,1},{8,14},{10,12},{12... | collective-permute-start | bytes 442376 | tf_op jit(solution)/shard_map/ppermute | solution.py:429
  22.2 11.8 %collective-permute-start.4 = (bf16[64,1152]{1,0:T(8,128)(2,1)S(1)}, bf16[64,1152]{1,0:T(8,128)(2,1)S(1)}, u32[]{:S(2)}, u32[]{:S(2)}) collective-permute-start(bf16[64,1152]{1,0:T(8,128)(2,1)S(1)} %get-tuple-element.45), channel_id=1, source_target_pairs={{0,4},{2,6},{4,0},{6,2},{1,5},{3,7},{5,1},{7,3},{8,12},{10,14},{12... | collective-permute-start | bytes 442376 | tf_op jit(solution)/shard_map/ppermute | solution.py:429
  23.4 10.7 %collective-permute-start.5 = (bf16[64,1152]{1,0:T(8,128)(2,1)S(1)}, bf16[64,1152]{1,0:T(8,128)(2,1)S(1)}, u32[]{:S(2)}, u32[]{:S(2)}) collective-permute-start(bf16[64,1152]{1,0:T(8,128)(2,1)S(1)} %get-tuple-element.46), channel_id=1, source_target_pairs={{0,2},{2,0},{4,6},{6,4},{1,3},{3,1},{5,7},{7,5},{8,10},{10,8},{12,... | collective-permute-start | bytes 442376 | tf_op jit(solution)/shard_map/ppermute | solution.py:429
  24.3 5.9 %collective-permute-start.11 = (bf16[64,1024]{1,0:T(8,128)(2,1)S(1)}, bf16[64,1024]{1,0:T(8,128)(2,1)S(1)}, u32[]{:S(2)}, u32[]{:S(2)}) collective-permute-start(bf16[64,1024]{1,0:T(8,128)(2,1)S(1)} %get-tuple-element.54), channel_id=1, source_target_pairs={{0,24},{8,16},{16,8},{24,0},{1,25},{9,17},{17,9},{25,1},{2,26},{10... | collective-permute-start | bytes 393224 | tf_op jit(solution)/shard_map/ppermute | solution.py:429
  25.8 5.0 %collective-permute-start.9 = (bf16[64,1024]{1,0:T(8,128)(2,1)S(1)}, bf16[64,1024]{1,0:T(8,128)(2,1)S(1)}, u32[]{:S(2)}, u32[]{:S(2)}) collective-permute-start(bf16[64,1024]{1,0:T(8,128)(2,1)S(1)} %get-tuple-element.52), channel_id=1, source_target_pairs={{0,8},{8,0},{16,24},{24,16},{1,9},{9,1},{17,25},{25,17},{2,10},{10... | collective-permute-start | bytes 393224 | tf_op jit(solution)/shard_map/ppermute | solution.py:429
  35.2 3.3 %collective-permute-start.15 = (bf16[8,32,512]{2,1,0:T(8,128)(2,1)S(1)}, bf16[8,32,512]{2,1,0:T(8,128)(2,1)S(1)}, u32[]{:S(2)}, u32[]{:S(2)}) collective-permute-start(bf16[8,32,512]{2,1,0:T(8,128)(2,1)S(1)} %get-tuple-element.59.refs_3_), channel_id=1, source_target_pairs={{0,1},{1,0},{2,3},{3,2},{4,5},{5,4},{6,7},{7,6},{8,9},{9,8},{10,11... | collective-permute-start | bytes 786440 | tf_op jit(solution)/shard_map/ppermute | solution.py:480
  35.3 15.9 %collective-permute-start.12 = (bf16[8,32,512]{2,1,0:T(8,128)(2,1)S(1)}, bf16[8,32,512]{2,1,0:T(8,128)(2,1)S(1)}, u32[]{:S(2)}, u32[]{:S(2)}) collective-permute-start(bf16[8,32,512]{2,1,0:T(8,128)(2,1)S(1)} %get-tuple-element.57.refs_0_), channel_id=1, source_target_pairs={{0,2},{2,0},{4,6},{6,4},{1,3},{3,1},{5,7},{7,5},{8,10},{10,8},{12,... | collective-permute-start | bytes 786440 | tf_op jit(solution)/shard_map/ppermute | solution.py:460
  35.4 15.5 %collective-permute-start.13 = (bf16[8,32,512]{2,1,0:T(8,128)(2,1)S(1)}, bf16[8,32,512]{2,1,0:T(8,128)(2,1)S(1)}, u32[]{:S(2)}, u32[]{:S(2)}) collective-permute-start(bf16[8,32,512]{2,1,0:T(8,128)(2,1)S(1)} %get-tuple-element.57.refs_0_), channel_id=1, source_target_pairs={{0,4},{2,6},{4,0},{6,2},{1,5},{3,7},{5,1},{7,3},{8,12},{10,14},{12... | collective-permute-start | bytes 786440 | tf_op jit(solution)/shard_map/ppermute | solution.py:460
  38.6 12.6 %collective-permute-start.18 = (bf16[8,32,512]{2,1,0:T(8,128)(2,1)S(1)}, bf16[8,32,512]{2,1,0:T(8,128)(2,1)S(1)}, u32[]{:S(2)}, u32[]{:S(2)}) collective-permute-start(bf16[8,32,512]{2,1,0:T(8,128)(2,1)S(1)} %get-tuple-element.59.refs_3_), channel_id=1, source_target_pairs={{0,24},{8,16},{16,8},{24,0},{1,25},{9,17},{17,9},{25,1},{2,26},{10... | collective-permute-start | bytes 786440 | tf_op jit(solution)/shard_map/ppermute | solution.py:405
  40.3 12.9 %collective-permute-start.17 = (bf16[8,32,512]{2,1,0:T(8,128)(2,1)S(1)}, bf16[8,32,512]{2,1,0:T(8,128)(2,1)S(1)}, u32[]{:S(2)}, u32[]{:S(2)}) collective-permute-start(bf16[8,32,512]{2,1,0:T(8,128)(2,1)S(1)} %get-tuple-element.59.refs_3_), channel_id=1, source_target_pairs={{0,16},{8,24},{16,0},{24,8},{1,17},{9,25},{17,1},{25,9},{2,18},{10... | collective-permute-start | bytes 786440 | tf_op jit(solution)/shard_map/ppermute | solution.py:405
  42.0 11.2 %collective-permute-start.16 = (bf16[8,32,512]{2,1,0:T(8,128)(2,1)S(1)}, bf16[8,32,512]{2,1,0:T(8,128)(2,1)S(1)}, u32[]{:S(2)}, u32[]{:S(2)}) collective-permute-start(bf16[8,32,512]{2,1,0:T(8,128)(2,1)S(1)} %get-tuple-element.59.refs_3_), channel_id=1, source_target_pairs={{0,8},{8,0},{16,24},{24,16},{1,9},{9,1},{17,25},{25,17},{2,10},{10... | collective-permute-start | bytes 786440 | tf_op jit(solution)/shard_map/ppermute | solution.py:405
  50.9 6.6 %collective-permute-start.14 = (bf16[8,32,512]{2,1,0:T(8,128)(2,1)S(1)}, bf16[8,32,512]{2,1,0:T(8,128)(2,1)S(1)}, u32[]{:S(2)}, u32[]{:S(2)}) collective-permute-start(bf16[8,32,512]{2,1,0:T(8,128)(2,1)S(1)} %collective-permute-done.13.refs_2_), channel_id=1, source_target_pairs={{0,2},{2,0},{4,6},{6,4},{1,3},{3,1},{5,7},{7,5},{8,10},{10,8},{12,... | collective-permute-start | bytes 786440 | tf_op jit(solution)/shard_map/ppermute | solution.py:460
  51.2 6.3 %collective-permute-start.21 = (bf16[8,32,512]{2,1,0:T(8,128)(2,1)S(1)}, bf16[8,32,512]{2,1,0:T(8,128)(2,1)S(1)}, u32[]{:S(2)}, u32[]{:S(2)}) collective-permute-start(bf16[8,32,512]{2,1,0:T(8,128)(2,1)S(1)} %collective-permute-done.18.refs_6_), channel_id=1, source_target_pairs={{0,1},{1,0},{2,3},{3,2},{4,5},{5,4},{6,7},{7,6},{8,9},{9,8},{10,11... | collective-permute-start | bytes 786440 | tf_op jit(solution)/shard_map/ppermute | solution.py:480
  53.2 4.3 %collective-permute-start.20 = (bf16[8,32,512]{2,1,0:T(8,128)(2,1)S(1)}, bf16[8,32,512]{2,1,0:T(8,128)(2,1)S(1)}, u32[]{:S(2)}, u32[]{:S(2)}) collective-permute-start(bf16[8,32,512]{2,1,0:T(8,128)(2,1)S(1)} %collective-permute-done.17.refs_5_), channel_id=1, source_target_pairs={{0,1},{1,0},{2,3},{3,2},{4,5},{5,4},{6,7},{7,6},{8,9},{9,8},{10,11... | collective-permute-start | bytes 786440 | tf_op jit(solution)/shard_map/ppermute | solution.py:480
  53.2 4.3 %collective-permute-start.19 = (bf16[8,32,512]{2,1,0:T(8,128)(2,1)S(1)}, bf16[8,32,512]{2,1,0:T(8,128)(2,1)S(1)}, u32[]{:S(2)}, u32[]{:S(2)}) collective-permute-start(bf16[8,32,512]{2,1,0:T(8,128)(2,1)S(1)} %collective-permute-done.16.refs_4_), channel_id=1, source_target_pairs={{0,1},{1,0},{2,3},{3,2},{4,5},{5,4},{6,7},{7,6},{8,9},{9,8},{10,11... | collective-permute-start | bytes 786440 | tf_op jit(solution)/shard_map/ppermute | solution.py:480
  58.2 6.5 %collective-permute-start.23 = (bf16[8,32,512]{2,1,0:T(8,128)(2,1)S(1)}, bf16[8,32,512]{2,1,0:T(8,128)(2,1)S(1)}, u32[]{:S(2)}, u32[]{:S(2)}) collective-permute-start(bf16[8,32,512]{2,1,0:T(8,128)(2,1)S(1)} %get-tuple-element.68.refs_6_), channel_id=1, source_target_pairs={{0,16},{8,24},{16,0},{24,8},{1,17},{9,25},{17,1},{25,9},{2,18},{10... | collective-permute-start | bytes 786440 | tf_op jit(solution)/shard_map/ppermute | solution.py:470
  59.7 7.8 %collective-permute-start.22 = (bf16[8,32,512]{2,1,0:T(8,128)(2,1)S(1)}, bf16[8,32,512]{2,1,0:T(8,128)(2,1)S(1)}, u32[]{:S(2)}, u32[]{:S(2)}) collective-permute-start(bf16[8,32,512]{2,1,0:T(8,128)(2,1)S(1)} %get-tuple-element.68.refs_6_), channel_id=1, source_target_pairs={{0,8},{8,0},{16,24},{24,16},{1,9},{9,1},{17,25},{25,17},{2,10},{10... | collective-permute-start | bytes 786440 | tf_op jit(solution)/shard_map/ppermute | solution.py:470
  60.5 7.6 %collective-permute-start.27 = (bf16[8,32,512]{2,1,0:T(8,128)(2,1)S(1)}, bf16[8,32,512]{2,1,0:T(8,128)(2,1)S(1)}, u32[]{:S(2)}, u32[]{:S(2)}) collective-permute-start(bf16[8,32,512]{2,1,0:T(8,128)(2,1)S(1)} %get-tuple-element.68.refs_6_), channel_id=1, source_target_pairs={{0,1},{1,0},{2,3},{3,2},{4,5},{5,4},{6,7},{7,6},{8,9},{9,8},{10,11... | collective-permute-start | bytes 786440 | tf_op jit(solution)/shard_map/ppermute | solution.py:480
  64.7 5.0 %collective-permute-start.25 = (bf16[4,32,512]{2,1,0:T(8,128)(2,1)S(1)}, bf16[4,32,512]{2,1,0:T(8,128)(2,1)S(1)}, u32[]{:S(2)}, u32[]{:S(2)}) collective-permute-start(bf16[4,32,512]{2,1,0:T(8,128)(2,1)S(1)} %slice.8), channel_id=1, source_target_pairs={{0,8},{8,0},{16,24},{24,16},{1,9},{9,1},{17,25},{25,17},{2,10},{10... | collective-permute-start | bytes 393224 | tf_op jit(solution)/shard_map/ppermute | solution.py:473
  67.5 5.0 %collective-permute-start.26 = (bf16[4,32,512]{2,1,0:T(8,128)(2,1)S(1)}, bf16[4,32,512]{2,1,0:T(8,128)(2,1)S(1)}, u32[]{:S(2)}, u32[]{:S(2)}) collective-permute-start(bf16[4,32,512]{2,1,0:T(8,128)(2,1)S(1)} %slice.9), channel_id=1, source_target_pairs={{0,16},{8,24},{16,0},{24,8},{1,17},{9,25},{17,1},{25,9},{2,18},{10... | collective-permute-start | bytes 393224 | tf_op jit(solution)/shard_map/ppermute | solution.py:474
  67.6 4.9 %collective-permute-start.29 = (bf16[8,32,512]{2,1,0:T(8,128)(2,1)S(1)}, bf16[8,32,512]{2,1,0:T(8,128)(2,1)S(1)}, u32[]{:S(2)}, u32[]{:S(2)}) collective-permute-start(bf16[8,32,512]{2,1,0:T(8,128)(2,1)S(1)} %collective-permute-done.23.refs_8_), channel_id=1, source_target_pairs={{0,1},{1,0},{2,3},{3,2},{4,5},{5,4},{6,7},{7,6},{8,9},{9,8},{10,11... | collective-permute-start | bytes 786440 | tf_op jit(solution)/shard_map/ppermute | solution.py:480
  67.6 4.9 %collective-permute-start.28 = (bf16[8,32,512]{2,1,0:T(8,128)(2,1)S(1)}, bf16[8,32,512]{2,1,0:T(8,128)(2,1)S(1)}, u32[]{:S(2)}, u32[]{:S(2)}) collective-permute-start(bf16[8,32,512]{2,1,0:T(8,128)(2,1)S(1)} %collective-permute-done.22.refs_7_), channel_id=1, source_target_pairs={{0,1},{1,0},{2,3},{3,2},{4,5},{5,4},{6,7},{7,6},{8,9},{9,8},{10,11... | collective-permute-start | bytes 786440 | tf_op jit(solution)/shard_map/ppermute | solution.py:480
  68.1 4.4 %collective-permute-start.24 = (bf16[4,4,32,512]{3,2,1,0:T(8,128)(2,1)S(1)}, bf16[4,4,32,512]{3,2,1,0:T(8,128)(2,1)S(1)}, u32[]{:S(2)}, u32[]{:S(2)}) collective-permute-start(bf16[4,4,32,512]{3,2,1,0:T(8,128)(2,1)S(1)} %get-tuple-element.69), channel_id=1, source_target_pairs={{0,1},{1,0},{2,3},{3,2},{4,5},{5,4},{6,7},{7,6},{8,9},{9,8},{10,11... | collective-permute-start | bytes 1572872 | tf_op jit(solution)/shard_map/ppermute | solution.py:480
  69.7 4.2 %collective-permute-start.30 = (bf16[4,32,512]{2,1,0:T(8,128)(2,1)S(1)}, bf16[4,32,512]{2,1,0:T(8,128)(2,1)S(1)}, u32[]{:S(2)}, u32[]{:S(2)}) collective-permute-start(bf16[4,32,512]{2,1,0:T(8,128)(2,1)S(1)} %collective-permute-done.25.refs_9_.refs_0_), channel_id=1, source_target_pairs={{0,1},{1,0},{2,3},{3,2},{4,5},{5,4},{6,7},{7,6},{8,9},{9,8},{10,11... | collective-permute-start | bytes 393224 | tf_op jit(solution)/shard_map/ppermute | solution.py:480
  72.5 1.4 %collective-permute-start.31 = (bf16[4,32,512]{2,1,0:T(8,128)(2,1)S(1)}, bf16[4,32,512]{2,1,0:T(8,128)(2,1)S(1)}, u32[]{:S(2)}, u32[]{:S(2)}) collective-permute-start(bf16[4,32,512]{2,1,0:T(8,128)(2,1)S(1)} %collective-permute-done.26.refs_10_.refs_1_), channel_id=1, source_target_pairs={{0,1},{1,0},{2,3},{3,2},{4,5},{5,4},{6,7},{7,6},{8,9},{9,8},{10,11... | collective-permute-start | bytes 393224 | tf_op jit(solution)/shard_map/ppermute | solution.py:480
  (5 other events, 12.4 us)
where the time goes:
time: 75.1 us; the launch traced here: 74.9 us
  waiting for transfers between devices  36.5 us (49%)
  starting transfers between devices  30.6 us (41%)
  Pallas kernels  6.91 us (9%)
    ppermute x3, waiting for transfers between devices, gather_line(): lax.ppermute(held, 'col', xor_pairs('col', step))  11.4 us
    ppermute x6, starting transfers between devices, relay(): lax.ppermute(parcel, out_axis, xor_pairs(out_axis, shift))  9.83 us
    ppermute x6, starting transfers between devices, relay(): lax.ppermute(parcel, in_axis, xor_pairs(in_axis, shift))  8.01 us
    ppermute x6, waiting for transfers between devices, relay(): lax.ppermute(parcel, in_axis, xor_pairs(in_axis, shift))  7.76 us
    ppermute x6, waiting for transfers between devices, relay(): lax.ppermute(parcel, out_axis, xor_pairs(out_axis, shift))  6.2 us
    ppermute x2, waiting for transfers between devices, gather_square(): lax.ppermute(piece, 'row', xor_pairs('row', shift))  4.87 us
    ppermute x3, starting transfers between devices, gather_line(): lax.ppermute(held, 'col', xor_pairs('col', step))  3.58 us
    ppermute x3, starting transfers between devices, gather(): lax.ppermute(piece, axis, xor_pairs(axis, shift))  3.49 us
  transfers between devices with their start and end apart: 32, of which 11 were waited for; matrix products, arithmetic and copies ran while one was open for 0% of the time, Pallas kernels for 3%

commit v1 on v0

--- a/solution.py
+++ b/solution.py
@@ -197,7 +197,7 @@
     values = []
     for twin in range(block_cols // 2):
         diagonal = jnp.where(row_id == col_start + twin * LANES + lane, occ, 0.0)
-        values.append(tall[twin] + diagonal)
+        values.append(tall[twin, :rows] + diagonal)
     here = slice(half * part_rows, (half + 1) * part_rows)
 
     def put(ref, at, value):
@@ -540,7 +540,9 @@
             out_shape=[piece_shape] * 2 if half else [marks_shape, half_shape, half_shape],
             in_specs=[whole_ref()] * (2 + len(blocks)),
             out_specs=[whole_ref()] * (2 if half else 3),
-            scratch_shapes=[pltpu.VMEM((cols // LANES, rows // 2, LANES), jnp.float32)],
+            scratch_shapes=[
+                pltpu.VMEM((cols // LANES, (rows + part_rows) // 2, LANES), jnp.float32)
+            ],
             compiler_params=params(2 * places * width + 8 * rows * cols),
             cost_estimate=cost(places * slots_here * part, places * width),
             name="build",

time: 75.1 us -> 75.1 us (level)
  no operation moved by 1% of the time
where the time goes in v1:
time: 75.1 us; the launch traced here: 74.9 us
  waiting for transfers between devices  36.5 us (49%)
  starting transfers between devices  30.6 us (41%)
  Pallas kernels  6.91 us (9%)
    ppermute x3, waiting for transfers between devices, gather_line(): lax.ppermute(held, 'col', xor_pairs('col', step))  11.4 us
    ppermute x6, starting transfers between devices, relay(): lax.ppermute(parcel, out_axis, xor_pairs(out_axis, shift))  9.83 us
    ppermute x6, starting transfers between devices, relay(): lax.ppermute(parcel, in_axis, xor_pairs(in_axis, shift))  8.01 us
    ppermute x6, waiting for transfers between devices, relay(): lax.ppermute(parcel, in_axis, xor_pairs(in_axis, shift))  7.76 us
    ppermute x6, waiting for transfers between devices, relay(): lax.ppermute(parcel, out_axis, xor_pairs(out_axis, shift))  6.2 us
    ppermute x2, waiting for transfers between devices, gather_square(): lax.ppermute(piece, 'row', xor_pairs('row', shift))  4.87 us
    ppermute x3, starting transfers between devices, gather_line(): lax.ppermute(held, 'col', xor_pairs('col', step))  3.58 us
    ppermute x3, starting transfers between devices, gather(): lax.ppermute(piece, axis, xor_pairs(axis, shift))  3.49 us
  transfers between devices with their start and end apart: 32, of which 11 were waited for; matrix products, arithmetic and copies ran while one was open for 0% of the time, Pallas kernels for 3%

profile of v1, /device:TPU:0, one launch (start us, length us, event | category | flops | bytes accessed | tf_op | source)
XLA Modules:
  0.0 74.9 jit_solution(5822991911395344348)
XLA Ops:
  0.0 0.7 copy-done.3
  0.7 1.5 %pack.1 = (bf16[64,1152]{1,0:T(8,128)(2,1)S(1)}, bf16[64,1152]{1,0:T(8,128)(2,1)S(1)}, bf16[64,1152]{1,0:T(8,128)(2,1)S(1)}, bf16[64,1152]{1,0:T(8,128)(2,1)S(1)...) custom-call(bf16[128,4096]{1,0:T(8,128)(2,1)} %tasks_ref.1, ...), custom_call_target="tpu_custom_call" | custom-call | flops 142606336 | bytes 1671168 | tf_op jit(solution)/shard_map/pack/pallas_call | solution.py:502
  2.2 3.1 %collective-permute-start.6 = (bf16[64,1024]{1,0:T(8,128)(2,1)S(1)}, bf16[64,1024]{1,0:T(8,128)(2,1)S(1)}, u32[]{:S(2)}, u32[]{:S(2)}) collective-permute-start(bf16[64,1024]{1,0:T(8,128)(2,1)S(1)} %get-tuple-element.49), channel_id=1, source_target_pairs={{0,2},{2,0},{4,6},{6,4},{1,3},{3,1},{5,7},{7,5},{8,10},{10,8},{12,... | collective-permute-start | bytes 393224 | tf_op jit(solution)/shard_map/ppermute | solution.py:413
  5.3 2.6 %collective-permute-start.7 = (bf16[64,1024]{1,0:T(8,128)(2,1)S(1)}, bf16[64,1024]{1,0:T(8,128)(2,1)S(1)}, u32[]{:S(2)}, u32[]{:S(2)}) collective-permute-start(bf16[64,1024]{1,0:T(8,128)(2,1)S(1)} %get-tuple-element.50), channel_id=1, source_target_pairs={{0,4},{2,6},{4,0},{6,2},{1,5},{3,7},{5,1},{7,3},{8,12},{10,14},{12... | collective-permute-start | bytes 393224 | tf_op jit(solution)/shard_map/ppermute | solution.py:413
  7.9 2.7 %collective-permute-start = (bf16[64,1152]{1,0:T(8,128)(2,1)S(1)}, bf16[64,1152]{1,0:T(8,128)(2,1)S(1)}, u32[]{:S(2)}, u32[]{:S(2)}) collective-permute-start(bf16[64,1152]{1,0:T(8,128)(2,1)S(1)} %get-tuple-element.40), channel_id=1, source_target_pairs={{0,24},{8,16},{16,8},{24,0},{1,25},{9,17},{17,9},{25,1},{2,26},{10... | collective-permute-start | bytes 442376 | tf_op jit(solution)/shard_map/ppermute | solution.py:413
  11.0 1.0 %collective-permute-start.2 = (bf16[64,1152]{1,0:T(8,128)(2,1)S(1)}, bf16[64,1152]{1,0:T(8,128)(2,1)S(1)}, u32[]{:S(2)}, u32[]{:S(2)}) collective-permute-start(bf16[64,1152]{1,0:T(8,128)(2,1)S(1)} %get-tuple-element.42), channel_id=1, source_target_pairs={{0,8},{8,0},{16,24},{24,16},{1,9},{9,1},{17,25},{25,17},{2,10},{10... | collective-permute-start | bytes 442376 | tf_op jit(solution)/shard_map/ppermute | solution.py:413
  12.0 6.2 %collective-permute-done.7.refs_1_.refs_2_.refs_5_ = bf16[64,1024]{1,0:T(8,128)(2,1)S(1)} collective-permute-done((bf16[64,1024]{1,0:T(8,128)(2,1)S(1)}, bf16[64,1024]{1,0:T(8,128)(2,1)S(1)}, u32[]{:S(2)}, u32[]{:S(2)}) %collective-permute-start.7) | collective-permute-done | bytes 131104 | tf_op jit(solution)/shard_map/ppermute | solution.py:413
  18.2 1.6 %collective-permute-start.10 = (bf16[64,1024]{1,0:T(8,128)(2,1)S(1)}, bf16[64,1024]{1,0:T(8,128)(2,1)S(1)}, u32[]{:S(2)}, u32[]{:S(2)}) collective-permute-start(bf16[64,1024]{1,0:T(8,128)(2,1)S(1)} %get-tuple-element.53), channel_id=1, source_target_pairs={{0,16},{8,24},{16,0},{24,8},{1,17},{9,25},{17,1},{25,9},{2,18},{10... | collective-permute-start | bytes 393224 | tf_op jit(solution)/shard_map/ppermute | solution.py:429
  19.9 2.4 %collective-permute-start.3 = (bf16[64,1152]{1,0:T(8,128)(2,1)S(1)}, bf16[64,1152]{1,0:T(8,128)(2,1)S(1)}, u32[]{:S(2)}, u32[]{:S(2)}) collective-permute-start(bf16[64,1152]{1,0:T(8,128)(2,1)S(1)} %get-tuple-element.44), channel_id=1, source_target_pairs={{0,6},{2,4},{4,2},{6,0},{1,7},{3,5},{5,3},{7,1},{8,14},{10,12},{12... | collective-permute-start | bytes 442376 | tf_op jit(solution)/shard_map/ppermute | solution.py:429
  22.2 1.1 %collective-permute-start.4 = (bf16[64,1152]{1,0:T(8,128)(2,1)S(1)}, bf16[64,1152]{1,0:T(8,128)(2,1)S(1)}, u32[]{:S(2)}, u32[]{:S(2)}) collective-permute-start(bf16[64,1152]{1,0:T(8,128)(2,1)S(1)} %get-tuple-element.45), channel_id=1, source_target_pairs={{0,4},{2,6},{4,0},{6,2},{1,5},{3,7},{5,1},{7,3},{8,12},{10,14},{12... | collective-permute-start | bytes 442376 | tf_op jit(solution)/shard_map/ppermute | solution.py:429
  23.4 1.0 %collective-permute-start.5 = (bf16[64,1152]{1,0:T(8,128)(2,1)S(1)}, bf16[64,1152]{1,0:T(8,128)(2,1)S(1)}, u32[]{:S(2)}, u32[]{:S(2)}) collective-permute-start(bf16[64,1152]{1,0:T(8,128)(2,1)S(1)} %get-tuple-element.46), channel_id=1, source_target_pairs={{0,2},{2,0},{4,6},{6,4},{1,3},{3,1},{5,7},{7,5},{8,10},{10,8},{12,... | collective-permute-start | bytes 442376 | tf_op jit(solution)/shard_map/ppermute | solution.py:429
  24.3 1.4 %collective-permute-start.11 = (bf16[64,1024]{1,0:T(8,128)(2,1)S(1)}, bf16[64,1024]{1,0:T(8,128)(2,1)S(1)}, u32[]{:S(2)}, u32[]{:S(2)}) collective-permute-start(bf16[64,1024]{1,0:T(8,128)(2,1)S(1)} %get-tuple-element.54), channel_id=1, source_target_pairs={{0,24},{8,16},{16,8},{24,0},{1,25},{9,17},{17,9},{25,1},{2,26},{10... | collective-permute-start | bytes 393224 | tf_op jit(solution)/shard_map/ppermute | solution.py:429
  26.3 3.9 %collective-permute-done.11.refs_6_.refs_1_ = bf16[64,1024]{1,0:T(8,128)(2,1)S(1)} collective-permute-done((bf16[64,1024]{1,0:T(8,128)(2,1)S(1)}, bf16[64,1024]{1,0:T(8,128)(2,1)S(1)}, u32[]{:S(2)}, u32[]{:S(2)}) %collective-permute-start.11) | collective-permute-done | bytes 131104 | tf_op jit(solution)/shard_map/ppermute | solution.py:429
  30.7 3.3 %collective-permute-done.4.refs_1_ = bf16[64,1152]{1,0:T(8,128)(2,1)S(1)} collective-permute-done((bf16[64,1152]{1,0:T(8,128)(2,1)S(1)}, bf16[64,1152]{1,0:T(8,128)(2,1)S(1)}, u32[]{:S(2)}, u32[]{:S(2)}) %collective-permute-start.4) | collective-permute-done | bytes 147488 | tf_op jit(solution)/shard_map/ppermute | solution.py:429
  34.1 0.6 build.2
  35.4 3.2 %collective-permute-start.13 = (bf16[8,32,512]{2,1,0:T(8,128)(2,1)S(1)}, bf16[8,32,512]{2,1,0:T(8,128)(2,1)S(1)}, u32[]{:S(2)}, u32[]{:S(2)}) collective-permute-start(bf16[8,32,512]{2,1,0:T(8,128)(2,1)S(1)} %get-tuple-element.57.refs_0_), channel_id=1, source_target_pairs={{0,4},{2,6},{4,0},{6,2},{1,5},{3,7},{5,1},{7,3},{8,12},{10,14},{12... | collective-permute-start | bytes 786440 | tf_op jit(solution)/shard_map/ppermute | solution.py:460
  38.6 1.7 %collective-permute-start.18 = (bf16[8,32,512]{2,1,0:T(8,128)(2,1)S(1)}, bf16[8,32,512]{2,1,0:T(8,128)(2,1)S(1)}, u32[]{:S(2)}, u32[]{:S(2)}) collective-permute-start(bf16[8,32,512]{2,1,0:T(8,128)(2,1)S(1)} %get-tuple-element.59.refs_3_), channel_id=1, source_target_pairs={{0,24},{8,16},{16,8},{24,0},{1,25},{9,17},{17,9},{25,1},{2,26},{10... | collective-permute-start | bytes 786440 | tf_op jit(solution)/shard_map/ppermute | solution.py:405
  40.3 1.7 %collective-permute-start.17 = (bf16[8,32,512]{2,1,0:T(8,128)(2,1)S(1)}, bf16[8,32,512]{2,1,0:T(8,128)(2,1)S(1)}, u32[]{:S(2)}, u32[]{:S(2)}) collective-permute-start(bf16[8,32,512]{2,1,0:T(8,128)(2,1)S(1)} %get-tuple-element.59.refs_3_), channel_id=1, source_target_pairs={{0,16},{8,24},{16,0},{24,8},{1,17},{9,25},{17,1},{25,9},{2,18},{10... | collective-permute-start | bytes 786440 | tf_op jit(solution)/shard_map/ppermute | solution.py:405
  42.1 8.8 %collective-permute-done.13.refs_2_ = bf16[8,32,512]{2,1,0:T(8,128)(2,1)S(1)} collective-permute-done((bf16[8,32,512]{2,1,0:T(8,128)(2,1)S(1)}, bf16[8,32,512]{2,1,0:T(8,128)(2,1)S(1)}, u32[]{:S(2)}, u32[]{:S(2)}) %collective-permute-start.13) | collective-permute-done | bytes 262176 | tf_op jit(solution)/shard_map/ppermute | solution.py:460
  51.2 2.0 %collective-permute-done.17.refs_5_ = bf16[8,32,512]{2,1,0:T(8,128)(2,1)S(1)} collective-permute-done((bf16[8,32,512]{2,1,0:T(8,128)(2,1)S(1)}, bf16[8,32,512]{2,1,0:T(8,128)(2,1)S(1)}, u32[]{:S(2)}, u32[]{:S(2)}) %collective-permute-start.17) | collective-permute-done | bytes 262176 | tf_op jit(solution)/shard_map/ppermute | solution.py:405
  53.7 1.2 %near_square.1 = (f32[256,512]{1,0:T(8,128)S(1)}, bf16[4,256,256]{2,1,0:T(8,128)(2,1)S(1)}, bf16[1,256,512]{2,1,0:T(8,128)(2,1)S(1)}, bf16[4,4,32,512]{3,2,1,0:T(8,128)(2,1)S(1)}) custom-call(bf16[8,32,512]{2,1,0:T(8,128)(2,1)S(1)} %get-tuple-element.57.refs_0_, bf16[8,32,512]{2,1,0:T(8,128)(2,1)S(1)} %collective-permute-done.12.refs_1_, ...), custom_call_target="tpu_custom_call" | custom-call | tf_op jit(solution)/shard_map/near_square/pallas_call | solution.py:568
  54.9 2.6 %collective-permute-done.14.refs_7_.refs_3_ = bf16[8,32,512]{2,1,0:T(8,128)(2,1)S(1)} collective-permute-done((bf16[8,32,512]{2,1,0:T(8,128)(2,1)S(1)}, bf16[8,32,512]{2,1,0:T(8,128)(2,1)S(1)}, u32[]{:S(2)}, u32[]{:S(2)}) %collective-permute-start.14) | collective-permute-done | bytes 262176 | tf_op jit(solution)/shard_map/ppermute | solution.py:460
  57.5 0.7 far_square.1
  58.2 1.5 %collective-permute-start.23 = (bf16[8,32,512]{2,1,0:T(8,128)(2,1)S(1)}, bf16[8,32,512]{2,1,0:T(8,128)(2,1)S(1)}, u32[]{:S(2)}, u32[]{:S(2)}) collective-permute-start(bf16[8,32,512]{2,1,0:T(8,128)(2,1)S(1)} %get-tuple-element.68.refs_6_), channel_id=1, source_target_pairs={{0,16},{8,24},{16,0},{24,8},{1,17},{9,25},{17,1},{25,9},{2,18},{10... | collective-permute-start | bytes 786440 | tf_op jit(solution)/shard_map/ppermute | solution.py:470
  59.7 0.9 %collective-permute-start.22 = (bf16[8,32,512]{2,1,0:T(8,128)(2,1)S(1)}, bf16[8,32,512]{2,1,0:T(8,128)(2,1)S(1)}, u32[]{:S(2)}, u32[]{:S(2)}) collective-permute-start(bf16[8,32,512]{2,1,0:T(8,128)(2,1)S(1)} %get-tuple-element.68.refs_6_), channel_id=1, source_target_pairs={{0,8},{8,0},{16,24},{24,16},{1,9},{9,1},{17,25},{25,17},{2,10},{10... | collective-permute-start | bytes 786440 | tf_op jit(solution)/shard_map/ppermute | solution.py:470
  60.5 4.1 %collective-permute-done.23.refs_8_ = bf16[8,32,512]{2,1,0:T(8,128)(2,1)S(1)} collective-permute-done((bf16[8,32,512]{2,1,0:T(8,128)(2,1)S(1)}, bf16[8,32,512]{2,1,0:T(8,128)(2,1)S(1)}, u32[]{:S(2)}, u32[]{:S(2)}) %collective-permute-start.23) | collective-permute-done | bytes 262176 | tf_op jit(solution)/shard_map/ppermute | solution.py:470
  64.7 2.0 %collective-permute-start.25 = (bf16[4,32,512]{2,1,0:T(8,128)(2,1)S(1)}, bf16[4,32,512]{2,1,0:T(8,128)(2,1)S(1)}, u32[]{:S(2)}, u32[]{:S(2)}) collective-permute-start(bf16[4,32,512]{2,1,0:T(8,128)(2,1)S(1)} %slice.8), channel_id=1, source_target_pairs={{0,8},{8,0},{16,24},{24,16},{1,9},{9,1},{17,25},{25,17},{2,10},{10... | collective-permute-start | bytes 393224 | tf_op jit(solution)/shard_map/ppermute | solution.py:473
  66.7 0.8 %collective-permute-done.22.refs_7_ = bf16[8,32,512]{2,1,0:T(8,128)(2,1)S(1)} collective-permute-done((bf16[8,32,512]{2,1,0:T(8,128)(2,1)S(1)}, bf16[8,32,512]{2,1,0:T(8,128)(2,1)S(1)}, u32[]{:S(2)}, u32[]{:S(2)}) %collective-permute-start.22) | collective-permute-done | bytes 262176 | tf_op jit(solution)/shard_map/ppermute | solution.py:470
  68.2 1.5 %collective-permute-done.25.refs_9_.refs_0_ = bf16[4,32,512]{2,1,0:T(8,128)(2,1)S(1)} collective-permute-done((bf16[4,32,512]{2,1,0:T(8,128)(2,1)S(1)}, bf16[4,32,512]{2,1,0:T(8,128)(2,1)S(1)}, u32[]{:S(2)}, u32[]{:S(2)}) %collective-permute-start.25) | collective-permute-done | bytes 131104 | tf_op jit(solution)/shard_map/ppermute | solution.py:473
  69.7 2.8 %collective-permute-done.26.refs_10_.refs_1_ = bf16[4,32,512]{2,1,0:T(8,128)(2,1)S(1)} collective-permute-done((bf16[4,32,512]{2,1,0:T(8,128)(2,1)S(1)}, bf16[4,32,512]{2,1,0:T(8,128)(2,1)S(1)}, u32[]{:S(2)}, u32[]{:S(2)}) %collective-permute-start.26) | collective-permute-done | bytes 131104 | tf_op jit(solution)/shard_map/ppermute | solution.py:474
  72.6 1.3 %near_cube.1 = (f32[256,512]{1,0:T(8,128)S(1)}, bf16[256,512]{1,0:T(8,128)(2,1)S(1)}, bf16[256,256]{1,0:T(8,128)(2,1)S(1)}) custom-call(bf16[8,32,512]{2,1,0:T(8,128)(2,1)S(1)} %get-tuple-element.57.refs_0_, bf16[8,32,512]{2,1,0:T(8,128)(2,1)S(1)} %collective-permute-done.12.refs_1_, bf16[8,32,512]{2,1,0:T(8,128)(2,1)S(1)} %collective-permute-done.13.refs_2_, ...), custom_call_target="tpu_custom_call" | custom-call | tf_op jit(solution)/shard_map/near_cube/pallas_call | solution.py:600
  73.9 1.0 %far_cube.1 = f32[256,512]{1,0:T(8,128)} custom-call(f32[256,512]{1,0:T(8,128)S(1)} %get-tuple-element.72.sum_ref, bf16[256,512]{1,0:T(8,128)(2,1)S(1)} %get-tuple-element.73.mask_ref, bf16[256,256]{1,0:T(8,128)(2,1)S(1)} %get-tuple-element.74.left_ref, bf16[4,32,512]{2,1,0:T(8,128)(2,1)S(1)} %collective-permute-done.30.refs_0_, ...), custom_call_target="tpu_custom_call" | custom-call | flops 268435456 | bytes 4194304 | tf_op jit(solution)/shard_map/far_cube/pallas_call | solution.py:618
  (55 shorter events, 4.0 us)
Async XLA Ops:
  2.2 8.9 %collective-permute-start.6 = (bf16[64,1024]{1,0:T(8,128)(2,1)S(1)}, bf16[64,1024]{1,0:T(8,128)(2,1)S(1)}, u32[]{:S(2)}, u32[]{:S(2)}) collective-permute-start(bf16[64,1024]{1,0:T(8,128)(2,1)S(1)} %get-tuple-element.49), channel_id=1, source_target_pairs={{0,2},{2,0},{4,6},{6,4},{1,3},{3,1},{5,7},{7,5},{8,10},{10,8},{12,... | collective-permute-start | bytes 393224 | tf_op jit(solution)/shard_map/ppermute | solution.py:413
  5.3 12.9 %collective-permute-start.7 = (bf16[64,1024]{1,0:T(8,128)(2,1)S(1)}, bf16[64,1024]{1,0:T(8,128)(2,1)S(1)}, u32[]{:S(2)}, u32[]{:S(2)}) collective-permute-start(bf16[64,1024]{1,0:T(8,128)(2,1)S(1)} %get-tuple-element.50), channel_id=1, source_target_pairs={{0,4},{2,6},{4,0},{6,2},{1,5},{3,7},{5,1},{7,3},{8,12},{10,14},{12... | collective-permute-start | bytes 393224 | tf_op jit(solution)/shard_map/ppermute | solution.py:413
  7.9 10.3 %collective-permute-start.8 = (bf16[64,1024]{1,0:T(8,128)(2,1)S(1)}, bf16[64,1024]{1,0:T(8,128)(2,1)S(1)}, u32[]{:S(2)}, u32[]{:S(2)}) collective-permute-start(bf16[64,1024]{1,0:T(8,128)(2,1)S(1)} %get-tuple-element.51), channel_id=1, source_target_pairs={{0,6},{2,4},{4,2},{6,0},{1,7},{3,5},{5,3},{7,1},{8,14},{10,12},{12... | collective-permute-start | bytes 393224 | tf_op jit(solution)/shard_map/ppermute | solution.py:413
  7.9 12.0 %collective-permute-start = (bf16[64,1152]{1,0:T(8,128)(2,1)S(1)}, bf16[64,1152]{1,0:T(8,128)(2,1)S(1)}, u32[]{:S(2)}, u32[]{:S(2)}) collective-permute-start(bf16[64,1152]{1,0:T(8,128)(2,1)S(1)} %get-tuple-element.40), channel_id=1, source_target_pairs={{0,24},{8,16},{16,8},{24,0},{1,25},{9,17},{17,9},{25,1},{2,26},{10... | collective-permute-start | bytes 442376 | tf_op jit(solution)/shard_map/ppermute | solution.py:413
  10.5 9.3 %collective-permute-start.1 = (bf16[64,1152]{1,0:T(8,128)(2,1)S(1)}, bf16[64,1152]{1,0:T(8,128)(2,1)S(1)}, u32[]{:S(2)}, u32[]{:S(2)}) collective-permute-start(bf16[64,1152]{1,0:T(8,128)(2,1)S(1)} %get-tuple-element.41), channel_id=1, source_target_pairs={{0,16},{8,24},{16,0},{24,8},{1,17},{9,25},{17,1},{25,9},{2,18},{10... | collective-permute-start | bytes 442376 | tf_op jit(solution)/shard_map/ppermute | solution.py:413
  11.0 8.8 %collective-permute-start.2 = (bf16[64,1152]{1,0:T(8,128)(2,1)S(1)}, bf16[64,1152]{1,0:T(8,128)(2,1)S(1)}, u32[]{:S(2)}, u32[]{:S(2)}) collective-permute-start(bf16[64,1152]{1,0:T(8,128)(2,1)S(1)} %get-tuple-element.42), channel_id=1, source_target_pairs={{0,8},{8,0},{16,24},{24,16},{1,9},{9,1},{17,25},{25,17},{2,10},{10... | collective-permute-start | bytes 442376 | tf_op jit(solution)/shard_map/ppermute | solution.py:413
  18.2 7.5 %collective-permute-start.10 = (bf16[64,1024]{1,0:T(8,128)(2,1)S(1)}, bf16[64,1024]{1,0:T(8,128)(2,1)S(1)}, u32[]{:S(2)}, u32[]{:S(2)}) collective-permute-start(bf16[64,1024]{1,0:T(8,128)(2,1)S(1)} %get-tuple-element.53), channel_id=1, source_target_pairs={{0,16},{8,24},{16,0},{24,8},{1,17},{9,25},{17,1},{25,9},{2,18},{10... | collective-permute-start | bytes 393224 | tf_op jit(solution)/shard_map/ppermute | solution.py:429
  19.9 10.9 %collective-permute-start.3 = (bf16[64,1152]{1,0:T(8,128)(2,1)S(1)}, bf16[64,1152]{1,0:T(8,128)(2,1)S(1)}, u32[]{:S(2)}, u32[]{:S(2)}) collective-permute-start(bf16[64,1152]{1,0:T(8,128)(2,1)S(1)} %get-tuple-element.44), channel_id=1, source_target_pairs={{0,6},{2,4},{4,2},{6,0},{1,7},{3,5},{5,3},{7,1},{8,14},{10,12},{12... | collective-permute-start | bytes 442376 | tf_op jit(solution)/shard_map/ppermute | solution.py:429
  22.2 11.8 %collective-permute-start.4 = (bf16[64,1152]{1,0:T(8,128)(2,1)S(1)}, bf16[64,1152]{1,0:T(8,128)(2,1)S(1)}, u32[]{:S(2)}, u32[]{:S(2)}) collective-permute-start(bf16[64,1152]{1,0:T(8,128)(2,1)S(1)} %get-tuple-element.45), channel_id=1, source_target_pairs={{0,4},{2,6},{4,0},{6,2},{1,5},{3,7},{5,1},{7,3},{8,12},{10,14},{12... | collective-permute-start | bytes 442376 | tf_op jit(solution)/shard_map/ppermute | solution.py:429
  23.4 10.7 %collective-permute-start.5 = (bf16[64,1152]{1,0:T(8,128)(2,1)S(1)}, bf16[64,1152]{1,0:T(8,128)(2,1)S(1)}, u32[]{:S(2)}, u32[]{:S(2)}) collective-permute-start(bf16[64,1152]{1,0:T(8,128)(2,1)S(1)} %get-tuple-element.46), channel_id=1, source_target_pairs={{0,2},{2,0},{4,6},{6,4},{1,3},{3,1},{5,7},{7,5},{8,10},{10,8},{12,... | collective-permute-start | bytes 442376 | tf_op jit(solution)/shard_map/ppermute | solution.py:429
  24.3 5.9 %collective-permute-start.11 = (bf16[64,1024]{1,0:T(8,128)(2,1)S(1)}, bf16[64,1024]{1,0:T(8,128)(2,1)S(1)}, u32[]{:S(2)}, u32[]{:S(2)}) collective-permute-start(bf16[64,1024]{1,0:T(8,128)(2,1)S(1)} %get-tuple-element.54), channel_id=1, source_target_pairs={{0,24},{8,16},{16,8},{24,0},{1,25},{9,17},{17,9},{25,1},{2,26},{10... | collective-permute-start | bytes 393224 | tf_op jit(solution)/shard_map/ppermute | solution.py:429
  25.8 5.0 %collective-permute-start.9 = (bf16[64,1024]{1,0:T(8,128)(2,1)S(1)}, bf16[64,1024]{1,0:T(8,128)(2,1)S(1)}, u32[]{:S(2)}, u32[]{:S(2)}) collective-permute-start(bf16[64,1024]{1,0:T(8,128)(2,1)S(1)} %get-tuple-element.52), channel_id=1, source_target_pairs={{0,8},{8,0},{16,24},{24,16},{1,9},{9,1},{17,25},{25,17},{2,10},{10... | collective-permute-start | bytes 393224 | tf_op jit(solution)/shard_map/ppermute | solution.py:429
  35.2 3.3 %collective-permute-start.15 = (bf16[8,32,512]{2,1,0:T(8,128)(2,1)S(1)}, bf16[8,32,512]{2,1,0:T(8,128)(2,1)S(1)}, u32[]{:S(2)}, u32[]{:S(2)}) collective-permute-start(bf16[8,32,512]{2,1,0:T(8,128)(2,1)S(1)} %get-tuple-element.59.refs_3_), channel_id=1, source_target_pairs={{0,1},{1,0},{2,3},{3,2},{4,5},{5,4},{6,7},{7,6},{8,9},{9,8},{10,11... | collective-permute-start | bytes 786440 | tf_op jit(solution)/shard_map/ppermute | solution.py:480
  35.3 15.9 %collective-permute-start.12 = (bf16[8,32,512]{2,1,0:T(8,128)(2,1)S(1)}, bf16[8,32,512]{2,1,0:T(8,128)(2,1)S(1)}, u32[]{:S(2)}, u32[]{:S(2)}) collective-permute-start(bf16[8,32,512]{2,1,0:T(8,128)(2,1)S(1)} %get-tuple-element.57.refs_0_), channel_id=1, source_target_pairs={{0,2},{2,0},{4,6},{6,4},{1,3},{3,1},{5,7},{7,5},{8,10},{10,8},{12,... | collective-permute-start | bytes 786440 | tf_op jit(solution)/shard_map/ppermute | solution.py:460
  35.4 15.5 %collective-permute-start.13 = (bf16[8,32,512]{2,1,0:T(8,128)(2,1)S(1)}, bf16[8,32,512]{2,1,0:T(8,128)(2,1)S(1)}, u32[]{:S(2)}, u32[]{:S(2)}) collective-permute-start(bf16[8,32,512]{2,1,0:T(8,128)(2,1)S(1)} %get-tuple-element.57.refs_0_), channel_id=1, source_target_pairs={{0,4},{2,6},{4,0},{6,2},{1,5},{3,7},{5,1},{7,3},{8,12},{10,14},{12... | collective-permute-start | bytes 786440 | tf_op jit(solution)/shard_map/ppermute | solution.py:460
  38.6 12.6 %collective-permute-start.18 = (bf16[8,32,512]{2,1,0:T(8,128)(2,1)S(1)}, bf16[8,32,512]{2,1,0:T(8,128)(2,1)S(1)}, u32[]{:S(2)}, u32[]{:S(2)}) collective-permute-start(bf16[8,32,512]{2,1,0:T(8,128)(2,1)S(1)} %get-tuple-element.59.refs_3_), channel_id=1, source_target_pairs={{0,24},{8,16},{16,8},{24,0},{1,25},{9,17},{17,9},{25,1},{2,26},{10... | collective-permute-start | bytes 786440 | tf_op jit(solution)/shard_map/ppermute | solution.py:405
  40.3 12.9 %collective-permute-start.17 = (bf16[8,32,512]{2,1,0:T(8,128)(2,1)S(1)}, bf16[8,32,512]{2,1,0:T(8,128)(2,1)S(1)}, u32[]{:S(2)}, u32[]{:S(2)}) collective-permute-start(bf16[8,32,512]{2,1,0:T(8,128)(2,1)S(1)} %get-tuple-element.59.refs_3_), channel_id=1, source_target_pairs={{0,16},{8,24},{16,0},{24,8},{1,17},{9,25},{17,1},{25,9},{2,18},{10... | collective-permute-start | bytes 786440 | tf_op jit(solution)/shard_map/ppermute | solution.py:405
  42.0 11.2 %collective-permute-start.16 = (bf16[8,32,512]{2,1,0:T(8,128)(2,1)S(1)}, bf16[8,32,512]{2,1,0:T(8,128)(2,1)S(1)}, u32[]{:S(2)}, u32[]{:S(2)}) collective-permute-start(bf16[8,32,512]{2,1,0:T(8,128)(2,1)S(1)} %get-tuple-element.59.refs_3_), channel_id=1, source_target_pairs={{0,8},{8,0},{16,24},{24,16},{1,9},{9,1},{17,25},{25,17},{2,10},{10... | collective-permute-start | bytes 786440 | tf_op jit(solution)/shard_map/ppermute | solution.py:405
  50.9 6.6 %collective-permute-start.14 = (bf16[8,32,512]{2,1,0:T(8,128)(2,1)S(1)}, bf16[8,32,512]{2,1,0:T(8,128)(2,1)S(1)}, u32[]{:S(2)}, u32[]{:S(2)}) collective-permute-start(bf16[8,32,512]{2,1,0:T(8,128)(2,1)S(1)} %collective-permute-done.13.refs_2_), channel_id=1, source_target_pairs={{0,2},{2,0},{4,6},{6,4},{1,3},{3,1},{5,7},{7,5},{8,10},{10,8},{12,... | collective-permute-start | bytes 786440 | tf_op jit(solution)/shard_map/ppermute | solution.py:460
  51.2 6.3 %collective-permute-start.21 = (bf16[8,32,512]{2,1,0:T(8,128)(2,1)S(1)}, bf16[8,32,512]{2,1,0:T(8,128)(2,1)S(1)}, u32[]{:S(2)}, u32[]{:S(2)}) collective-permute-start(bf16[8,32,512]{2,1,0:T(8,128)(2,1)S(1)} %collective-permute-done.18.refs_6_), channel_id=1, source_target_pairs={{0,1},{1,0},{2,3},{3,2},{4,5},{5,4},{6,7},{7,6},{8,9},{9,8},{10,11... | collective-permute-start | bytes 786440 | tf_op jit(solution)/shard_map/ppermute | solution.py:480
  53.2 4.3 %collective-permute-start.20 = (bf16[8,32,512]{2,1,0:T(8,128)(2,1)S(1)}, bf16[8,32,512]{2,1,0:T(8,128)(2,1)S(1)}, u32[]{:S(2)}, u32[]{:S(2)}) collective-permute-start(bf16[8,32,512]{2,1,0:T(8,128)(2,1)S(1)} %collective-permute-done.17.refs_5_), channel_id=1, source_target_pairs={{0,1},{1,0},{2,3},{3,2},{4,5},{5,4},{6,7},{7,6},{8,9},{9,8},{10,11... | collective-permute-start | bytes 786440 | tf_op jit(solution)/shard_map/ppermute | solution.py:480
  53.2 4.3 %collective-permute-start.19 = (bf16[8,32,512]{2,1,0:T(8,128)(2,1)S(1)}, bf16[8,32,512]{2,1,0:T(8,128)(2,1)S(1)}, u32[]{:S(2)}, u32[]{:S(2)}) collective-permute-start(bf16[8,32,512]{2,1,0:T(8,128)(2,1)S(1)} %collective-permute-done.16.refs_4_), channel_id=1, source_target_pairs={{0,1},{1,0},{2,3},{3,2},{4,5},{5,4},{6,7},{7,6},{8,9},{9,8},{10,11... | collective-permute-start | bytes 786440 | tf_op jit(solution)/shard_map/ppermute | solution.py:480
  58.2 6.5 %collective-permute-start.23 = (bf16[8,32,512]{2,1,0:T(8,128)(2,1)S(1)}, bf16[8,32,512]{2,1,0:T(8,128)(2,1)S(1)}, u32[]{:S(2)}, u32[]{:S(2)}) collective-permute-start(bf16[8,32,512]{2,1,0:T(8,128)(2,1)S(1)} %get-tuple-element.68.refs_6_), channel_id=1, source_target_pairs={{0,16},{8,24},{16,0},{24,8},{1,17},{9,25},{17,1},{25,9},{2,18},{10... | collective-permute-start | bytes 786440 | tf_op jit(solution)/shard_map/ppermute | solution.py:470
  59.7 7.8 %collective-permute-start.22 = (bf16[8,32,512]{2,1,0:T(8,128)(2,1)S(1)}, bf16[8,32,512]{2,1,0:T(8,128)(2,1)S(1)}, u32[]{:S(2)}, u32[]{:S(2)}) collective-permute-start(bf16[8,32,512]{2,1,0:T(8,128)(2,1)S(1)} %get-tuple-element.68.refs_6_), channel_id=1, source_target_pairs={{0,8},{8,0},{16,24},{24,16},{1,9},{9,1},{17,25},{25,17},{2,10},{10... | collective-permute-start | bytes 786440 | tf_op jit(solution)/shard_map/ppermute | solution.py:470
  60.5 7.6 %collective-permute-start.27 = (bf16[8,32,512]{2,1,0:T(8,128)(2,1)S(1)}, bf16[8,32,512]{2,1,0:T(8,128)(2,1)S(1)}, u32[]{:S(2)}, u32[]{:S(2)}) collective-permute-start(bf16[8,32,512]{2,1,0:T(8,128)(2,1)S(1)} %get-tuple-element.68.refs_6_), channel_id=1, source_target_pairs={{0,1},{1,0},{2,3},{3,2},{4,5},{5,4},{6,7},{7,6},{8,9},{9,8},{10,11... | collective-permute-start | bytes 786440 | tf_op jit(solution)/shard_map/ppermute | solution.py:480
  64.7 5.0 %collective-permute-start.25 = (bf16[4,32,512]{2,1,0:T(8,128)(2,1)S(1)}, bf16[4,32,512]{2,1,0:T(8,128)(2,1)S(1)}, u32[]{:S(2)}, u32[]{:S(2)}) collective-permute-start(bf16[4,32,512]{2,1,0:T(8,128)(2,1)S(1)} %slice.8), channel_id=1, source_target_pairs={{0,8},{8,0},{16,24},{24,16},{1,9},{9,1},{17,25},{25,17},{2,10},{10... | collective-permute-start | bytes 393224 | tf_op jit(solution)/shard_map/ppermute | solution.py:473
  67.5 5.0 %collective-permute-start.26 = (bf16[4,32,512]{2,1,0:T(8,128)(2,1)S(1)}, bf16[4,32,512]{2,1,0:T(8,128)(2,1)S(1)}, u32[]{:S(2)}, u32[]{:S(2)}) collective-permute-start(bf16[4,32,512]{2,1,0:T(8,128)(2,1)S(1)} %slice.9), channel_id=1, source_target_pairs={{0,16},{8,24},{16,0},{24,8},{1,17},{9,25},{17,1},{25,9},{2,18},{10... | collective-permute-start | bytes 393224 | tf_op jit(solution)/shard_map/ppermute | solution.py:474
  67.6 4.9 %collective-permute-start.29 = (bf16[8,32,512]{2,1,0:T(8,128)(2,1)S(1)}, bf16[8,32,512]{2,1,0:T(8,128)(2,1)S(1)}, u32[]{:S(2)}, u32[]{:S(2)}) collective-permute-start(bf16[8,32,512]{2,1,0:T(8,128)(2,1)S(1)} %collective-permute-done.23.refs_8_), channel_id=1, source_target_pairs={{0,1},{1,0},{2,3},{3,2},{4,5},{5,4},{6,7},{7,6},{8,9},{9,8},{10,11... | collective-permute-start | bytes 786440 | tf_op jit(solution)/shard_map/ppermute | solution.py:480
  67.6 4.9 %collective-permute-start.28 = (bf16[8,32,512]{2,1,0:T(8,128)(2,1)S(1)}, bf16[8,32,512]{2,1,0:T(8,128)(2,1)S(1)}, u32[]{:S(2)}, u32[]{:S(2)}) collective-permute-start(bf16[8,32,512]{2,1,0:T(8,128)(2,1)S(1)} %collective-permute-done.22.refs_7_), channel_id=1, source_target_pairs={{0,1},{1,0},{2,3},{3,2},{4,5},{5,4},{6,7},{7,6},{8,9},{9,8},{10,11... | collective-permute-start | bytes 786440 | tf_op jit(solution)/shard_map/ppermute | solution.py:480
  68.1 4.4 %collective-permute-start.24 = (bf16[4,4,32,512]{3,2,1,0:T(8,128)(2,1)S(1)}, bf16[4,4,32,512]{3,2,1,0:T(8,128)(2,1)S(1)}, u32[]{:S(2)}, u32[]{:S(2)}) collective-permute-start(bf16[4,4,32,512]{3,2,1,0:T(8,128)(2,1)S(1)} %get-tuple-element.69), channel_id=1, source_target_pairs={{0,1},{1,0},{2,3},{3,2},{4,5},{5,4},{6,7},{7,6},{8,9},{9,8},{10,11... | collective-permute-start | bytes 1572872 | tf_op jit(solution)/shard_map/ppermute | solution.py:480
  69.7 4.2 %collective-permute-start.30 = (bf16[4,32,512]{2,1,0:T(8,128)(2,1)S(1)}, bf16[4,32,512]{2,1,0:T(8,128)(2,1)S(1)}, u32[]{:S(2)}, u32[]{:S(2)}) collective-permute-start(bf16[4,32,512]{2,1,0:T(8,128)(2,1)S(1)} %collective-permute-done.25.refs_9_.refs_0_), channel_id=1, source_target_pairs={{0,1},{1,0},{2,3},{3,2},{4,5},{5,4},{6,7},{7,6},{8,9},{9,8},{10,11... | collective-permute-start | bytes 393224 | tf_op jit(solution)/shard_map/ppermute | solution.py:480
  72.5 1.4 %collective-permute-start.31 = (bf16[4,32,512]{2,1,0:T(8,128)(2,1)S(1)}, bf16[4,32,512]{2,1,0:T(8,128)(2,1)S(1)}, u32[]{:S(2)}, u32[]{:S(2)}) collective-permute-start(bf16[4,32,512]{2,1,0:T(8,128)(2,1)S(1)} %collective-permute-done.26.refs_10_.refs_1_), channel_id=1, source_target_pairs={{0,1},{1,0},{2,3},{3,2},{4,5},{5,4},{6,7},{7,6},{8,9},{9,8},{10,11... | collective-permute-start | bytes 393224 | tf_op jit(solution)/shard_map/ppermute | solution.py:480
  (5 other events, 12.4 us)

commit v2 on v1

--- a/solution.py
+++ b/solution.py
@@ -275,7 +275,7 @@
     inner = len(pairs)
     here = give_ref.shape[1]
     pairs += [
-        (piece.at[pl.ds((1 - layer) * here, here)], give_ref.at[col ^ shift])
+        (piece.at[pl.ds((1 - layer) * here, here)], give_ref.at[shift])
         for shift, piece in enumerate(lefts)
     ]
     copies = start_copies(pairs, sems)
@@ -306,11 +306,11 @@
 def far_square_kernel(n_col, n_row, *refs):
     sum_ref, other_ref, met_ref = refs[:3]
     mates, left_ref = refs[3 : 3 + n_row], refs[3 + n_row]
-    low_ref, give_ref, sem = refs[5 + n_row :]
+    low_ref, give_ref, sem = refs[6 + n_row :]
     row, col, layer = (lax.axis_index(axis) for axis in ("row", "col", "layer"))
-    here = give_ref.shape[1]
+    here = give_ref.shape[0]
     copy = pltpu.make_async_copy(
-        left_ref.at[pl.ds((1 - layer) * here, here)], give_ref.at[col ^ (n_col - 1)], sem
+        left_ref.at[pl.ds((1 - layer) * here, here)], give_ref, sem
     )
     copy.start()
     per_col = met_ref.shape[0]
@@ -338,14 +338,15 @@
 
 
 def near_cube_kernel(n_col, sizes, *refs):
-    lefts, given, pattern_ref = refs[:n_col], refs[n_col], refs[n_col + 1]
-    n_row, count = len(sizes), n_col + 2 + sum(sizes)
-    pieces, mates = split(refs[n_col + 2 : count], sizes), refs[count : count + n_row - 1]
+    lefts, given, pattern_ref = refs[:n_col], refs[n_col : n_col + 2], refs[n_col + 2]
+    n_row, count = len(sizes), n_col + 3 + sum(sizes)
+    pieces, mates = split(refs[n_col + 3 : count], sizes), refs[count : count + n_row - 1]
     sum_ref, mask_ref, other_ref, left, own, sems = refs[count + n_row - 1 :]
     row, col, layer = (lax.axis_index(axis) for axis in ("row", "col", "layer"))
     rows, cols = sum_ref.shape
     per_col = n_row // n_col
-    here = given.shape[1]
+    here = given[1].shape[0]
+    given = [given[0].at[shift] for shift in range(n_col - 1)] + [given[1]]
     mine = pl.ds(layer * here, here)
     pairs = []
     for block, which, lanes in left_blocks(cols // per_col, cols):
@@ -353,7 +354,7 @@
             at = (col ^ shift) * per_col + block
             pairs.append((piece.at[mine, :, lanes], left.at[at, which, :, layer]))
             pairs.append(
-                (given.at[col ^ shift, :, :, lanes], left.at[at, which, :, 1 - layer])
+                (given[shift].at[:, :, lanes], left.at[at, which, :, 1 - layer])
             )
     copies = start_copies(pairs, sems)
     own[:, layer] = pieces[0][0][mine]
@@ -564,10 +565,15 @@
     other_shape = jax.ShapeDtypeStruct((n_row, rows, half_width), jnp.bfloat16)
     met_shape = jax.ShapeDtypeStruct((n_row // n_col, rows, cols), jnp.bfloat16)
     here = block_rows // layers
-    give_shape = jax.ShapeDtypeStruct((n_col, here, part_rows, cols), jnp.bfloat16)
+    give_shape = (here, part_rows, cols)
     partial, other, met, give = pl.pallas_call(
         functools.partial(near_square_kernel, n_col, n_row),
-        out_shape=[sum_shape, other_shape, met_shape, give_shape],
+        out_shape=[
+            sum_shape,
+            other_shape,
+            met_shape,
+            jax.ShapeDtypeStruct((n_col - 1, *give_shape), jnp.bfloat16),
+        ],
         in_specs=[any_ref()] * (n_col - 1) + [whole_ref()] * n_row,
         out_specs=[whole_ref()] * 3 + [any_ref()],
         scratch_shapes=[
@@ -578,23 +584,23 @@
         cost_estimate=cost(0, 0),
         name="near_square",
     )(*lefts[:-1], *pieces)
+    received = swap(give)
     square, give = pl.pallas_call(
         functools.partial(far_square_kernel, n_col, n_row),
-        out_shape=[piece_shape, give_shape],
-        in_specs=[whole_ref()] * (4 + n_row) + [any_ref()],
+        out_shape=[piece_shape, jax.ShapeDtypeStruct(give_shape, jnp.bfloat16)],
+        in_specs=[whole_ref()] * (4 + n_row) + [any_ref()] * 2,
         out_specs=[whole_ref(), any_ref()],
         scratch_shapes=[pltpu.SemaphoreType.DMA],
-        input_output_aliases={4 + n_row: 1},
         compiler_params=params(panel_bytes + 16 * rows * cols),
         cost_estimate=cost(0, 0),
         name="far_square",
-    )(partial, other, met, *mates, lefts[-1], give)
+    )(partial, other, met, *mates, lefts[-1], received, token(lefts[-1:], HEAVY))
 
     pieces = gather_square(square)
     mates = [[swap(part) for part in parts] for parts in pieces]
     if len(pieces[-1]) > 1:
         mates[1:3] = [[swap(after(pieces[shift][0], pieces[3 - shift][0]))] for shift in (1, 2)]
-    received = swap(after(give, pieces[1][0], pieces[2][0]))
+    received = [received, swap(after(give, pieces[1][0], pieces[2][0]))]
     sizes = [len(parts) for parts in pieces]
     pieces, mates = ([part for parts in held for part in parts] for held in (pieces, mates))
     partial, mask, other = pl.pallas_call(
@@ -604,7 +610,7 @@
             jax.ShapeDtypeStruct((rows, cols), jnp.bfloat16),
             jax.ShapeDtypeStruct((rows, half_width), jnp.bfloat16),
         ],
-        in_specs=[any_ref()] * (n_col + 1) + [whole_ref()] * (n_row + len(pieces)),
+        in_specs=[any_ref()] * (n_col + 2) + [whole_ref()] * (n_row + len(pieces)),
         out_specs=[whole_ref()] * 3,
         scratch_shapes=[
             pltpu.VMEM((n_row, layers, here, layers, part_rows, half_width), jnp.bfloat16),
@@ -614,7 +620,7 @@
         compiler_params=params(2 * panel_bytes + 16 * rows * cols),
         cost_estimate=cost(0, 0),
         name="near_cube",
-    )(*lefts, received, c_pattern, *pieces, *mates[: n_row - 1])
+    )(*lefts, *received, c_pattern, *pieces, *mates[: n_row - 1])
     return pl.pallas_call(
         far_cube_kernel,
         out_shape=sum_shape,

time: 75.1 us -> 75.4 us (level)
    ppermute x1, waiting for transfers between devices: 2.82 us -> 0.81 us  [gather_square(): lax.ppermute(one[middle:], 'row', xor_pairs('row', 2))]
    ppermute x1, starting transfers between devices: 2.03 us -> 0.58 us  [gather_square(): lax.ppermute(two[:middle], 'row', xor_pairs('row', 1))]
    ppermute x1, starting transfers between devices: 0.14 us -> 1.47 us  [gather_square(): lax.ppermute(one[middle:], 'row', xor_pairs('row', 2))]
    ppermute x3, waiting for transfers between devices: 1.99 us -> 2.8 us  [gather(): lax.ppermute(piece, axis, xor_pairs(axis, shift))]
    ppermute x2, waiting for transfers between devices: 4.87 us -> 5.64 us  [gather_square(): lax.ppermute(piece, 'row', xor_pairs('row', shift))]
    ppermute x1, waiting for transfers between devices: 1.47 us -> 2.23 us  [gather_square(): lax.ppermute(two[:middle], 'row', xor_pairs('row', 1))]
    ppermute x10 -> x11, starting transfers between devices: 1.18 us -> 1.67 us  [swap(): return lax.ppermute(piece, 'layer', xor_pairs('layer', 1))]
  transfers between devices with their start and end apart: 32 -> 33, of which waited for: 11 -> 13; matrix products, arithmetic and copies ran while one was open for 0% -> 0% of each run, Pallas kernels for 3% -> 3%
where the time goes in v2:
time: 75.4 us; the launch traced here: 75.2 us
  waiting for transfers between devices  37.1 us (49%)
  starting transfers between devices  30.3 us (40%)
  Pallas kernels  6.94 us (9%)
    ppermute x3, waiting for transfers between devices, gather_line(): lax.ppermute(held, 'col', xor_pairs('col', step))  11.6 us
    ppermute x6, starting transfers between devices, relay(): lax.ppermute(parcel, out_axis, xor_pairs(out_axis, shift))  9.83 us
    ppermute x6, starting transfers between devices, relay(): lax.ppermute(parcel, in_axis, xor_pairs(in_axis, shift))  8.01 us
    ppermute x6, waiting for transfers between devices, relay(): lax.ppermute(parcel, in_axis, xor_pairs(in_axis, shift))  7.74 us
    ppermute x6, waiting for transfers between devices, relay(): lax.ppermute(parcel, out_axis, xor_pairs(out_axis, shift))  6.2 us
    ppermute x2, waiting for transfers between devices, gather_square(): lax.ppermute(piece, 'row', xor_pairs('row', shift))  5.64 us
    ppermute x3, starting transfers between devices, gather(): lax.ppermute(piece, axis, xor_pairs(axis, shift))  3.49 us
    ppermute x3, starting transfers between devices, gather_line(): lax.ppermute(held, 'col', xor_pairs('col', step))  3.3 us
  transfers between devices with their start and end apart: 33, of which 13 were waited for; matrix products, arithmetic and copies ran while one was open for 0% of the time, Pallas kernels for 3%

profile of v2, /device:TPU:0, one launch (start us, length us, event | category | flops | bytes accessed | tf_op | source)
XLA Modules:
  0.0 75.2 jit_solution(7040375729881223634)
XLA Ops:
  0.0 0.7 copy-done.3
  0.7 1.5 %pack.1 = (bf16[64,1152]{1,0:T(8,128)(2,1)S(1)}, bf16[64,1152]{1,0:T(8,128)(2,1)S(1)}, bf16[64,1152]{1,0:T(8,128)(2,1)S(1)}, bf16[64,1152]{1,0:T(8,128)(2,1)S(1)...) custom-call(bf16[128,4096]{1,0:T(8,128)(2,1)} %tasks_ref.1, ...), custom_call_target="tpu_custom_call" | custom-call | flops 142606336 | bytes 1671168 | tf_op jit(solution)/shard_map/pack/pallas_call | solution.py:503
  2.2 3.1 %collective-permute-start.6 = (bf16[64,1024]{1,0:T(8,128)(2,1)S(1)}, bf16[64,1024]{1,0:T(8,128)(2,1)S(1)}, u32[]{:S(2)}, u32[]{:S(2)}) collective-permute-start(bf16[64,1024]{1,0:T(8,128)(2,1)S(1)} %get-tuple-element.49), channel_id=1, source_target_pairs={{0,2},{2,0},{4,6},{6,4},{1,3},{3,1},{5,7},{7,5},{8,10},{10,8},{12,... | collective-permute-start | bytes 393224 | tf_op jit(solution)/shard_map/ppermute | solution.py:414
  5.3 2.6 %collective-permute-start.7 = (bf16[64,1024]{1,0:T(8,128)(2,1)S(1)}, bf16[64,1024]{1,0:T(8,128)(2,1)S(1)}, u32[]{:S(2)}, u32[]{:S(2)}) collective-permute-start(bf16[64,1024]{1,0:T(8,128)(2,1)S(1)} %get-tuple-element.50), channel_id=1, source_target_pairs={{0,4},{2,6},{4,0},{6,2},{1,5},{3,7},{5,1},{7,3},{8,12},{10,14},{12... | collective-permute-start | bytes 393224 | tf_op jit(solution)/shard_map/ppermute | solution.py:414
  7.9 2.7 %collective-permute-start = (bf16[64,1152]{1,0:T(8,128)(2,1)S(1)}, bf16[64,1152]{1,0:T(8,128)(2,1)S(1)}, u32[]{:S(2)}, u32[]{:S(2)}) collective-permute-start(bf16[64,1152]{1,0:T(8,128)(2,1)S(1)} %get-tuple-element.40), channel_id=1, source_target_pairs={{0,24},{8,16},{16,8},{24,0},{1,25},{9,17},{17,9},{25,1},{2,26},{10... | collective-permute-start | bytes 442376 | tf_op jit(solution)/shard_map/ppermute | solution.py:414
  11.0 1.0 %collective-permute-start.2 = (bf16[64,1152]{1,0:T(8,128)(2,1)S(1)}, bf16[64,1152]{1,0:T(8,128)(2,1)S(1)}, u32[]{:S(2)}, u32[]{:S(2)}) collective-permute-start(bf16[64,1152]{1,0:T(8,128)(2,1)S(1)} %get-tuple-element.42), channel_id=1, source_target_pairs={{0,8},{8,0},{16,24},{24,16},{1,9},{9,1},{17,25},{25,17},{2,10},{10... | collective-permute-start | bytes 442376 | tf_op jit(solution)/shard_map/ppermute | solution.py:414
  12.0 6.2 %collective-permute-done.7.refs_1_.refs_2_.refs_5_ = bf16[64,1024]{1,0:T(8,128)(2,1)S(1)} collective-permute-done((bf16[64,1024]{1,0:T(8,128)(2,1)S(1)}, bf16[64,1024]{1,0:T(8,128)(2,1)S(1)}, u32[]{:S(2)}, u32[]{:S(2)}) %collective-permute-start.7) | collective-permute-done | bytes 131104 | tf_op jit(solution)/shard_map/ppermute | solution.py:414
  18.2 1.6 %collective-permute-start.9 = (bf16[64,1024]{1,0:T(8,128)(2,1)S(1)}, bf16[64,1024]{1,0:T(8,128)(2,1)S(1)}, u32[]{:S(2)}, u32[]{:S(2)}) collective-permute-start(bf16[64,1024]{1,0:T(8,128)(2,1)S(1)} %get-tuple-element.52), channel_id=1, source_target_pairs={{0,8},{8,0},{16,24},{24,16},{1,9},{9,1},{17,25},{25,17},{2,10},{10... | collective-permute-start | bytes 393224 | tf_op jit(solution)/shard_map/ppermute | solution.py:430
  19.8 2.4 %collective-permute-start.3 = (bf16[64,1152]{1,0:T(8,128)(2,1)S(1)}, bf16[64,1152]{1,0:T(8,128)(2,1)S(1)}, u32[]{:S(2)}, u32[]{:S(2)}) collective-permute-start(bf16[64,1152]{1,0:T(8,128)(2,1)S(1)} %get-tuple-element.44), channel_id=1, source_target_pairs={{0,6},{2,4},{4,2},{6,0},{1,7},{3,5},{5,3},{7,1},{8,14},{10,12},{12... | collective-permute-start | bytes 442376 | tf_op jit(solution)/shard_map/ppermute | solution.py:430
  22.2 1.1 %collective-permute-start.4 = (bf16[64,1152]{1,0:T(8,128)(2,1)S(1)}, bf16[64,1152]{1,0:T(8,128)(2,1)S(1)}, u32[]{:S(2)}, u32[]{:S(2)}) collective-permute-start(bf16[64,1152]{1,0:T(8,128)(2,1)S(1)} %get-tuple-element.45), channel_id=1, source_target_pairs={{0,4},{2,6},{4,0},{6,2},{1,5},{3,7},{5,1},{7,3},{8,12},{10,14},{12... | collective-permute-start | bytes 442376 | tf_op jit(solution)/shard_map/ppermute | solution.py:430
  23.3 1.0 %collective-permute-start.5 = (bf16[64,1152]{1,0:T(8,128)(2,1)S(1)}, bf16[64,1152]{1,0:T(8,128)(2,1)S(1)}, u32[]{:S(2)}, u32[]{:S(2)}) collective-permute-start(bf16[64,1152]{1,0:T(8,128)(2,1)S(1)} %get-tuple-element.46), channel_id=1, source_target_pairs={{0,2},{2,0},{4,6},{6,4},{1,3},{3,1},{5,7},{7,5},{8,10},{10,8},{12,... | collective-permute-start | bytes 442376 | tf_op jit(solution)/shard_map/ppermute | solution.py:430
  24.3 1.5 %collective-permute-start.10 = (bf16[64,1024]{1,0:T(8,128)(2,1)S(1)}, bf16[64,1024]{1,0:T(8,128)(2,1)S(1)}, u32[]{:S(2)}, u32[]{:S(2)}) collective-permute-start(bf16[64,1024]{1,0:T(8,128)(2,1)S(1)} %get-tuple-element.53), channel_id=1, source_target_pairs={{0,16},{8,24},{16,0},{24,8},{1,17},{9,25},{17,1},{25,9},{2,18},{10... | collective-permute-start | bytes 393224 | tf_op jit(solution)/shard_map/ppermute | solution.py:430
  26.3 3.0 %collective-permute-done.10.refs_5_.refs_2_ = bf16[64,1024]{1,0:T(8,128)(2,1)S(1)} collective-permute-done((bf16[64,1024]{1,0:T(8,128)(2,1)S(1)}, bf16[64,1024]{1,0:T(8,128)(2,1)S(1)}, u32[]{:S(2)}, u32[]{:S(2)}) %collective-permute-start.10) | collective-permute-done | bytes 131104 | tf_op jit(solution)/shard_map/ppermute | solution.py:430
  29.3 2.4 %collective-permute-done.11.refs_6_.refs_1_ = bf16[64,1024]{1,0:T(8,128)(2,1)S(1)} collective-permute-done((bf16[64,1024]{1,0:T(8,128)(2,1)S(1)}, bf16[64,1024]{1,0:T(8,128)(2,1)S(1)}, u32[]{:S(2)}, u32[]{:S(2)}) %collective-permute-start.11) | collective-permute-done | bytes 131104 | tf_op jit(solution)/shard_map/ppermute | solution.py:430
  31.7 2.3 %collective-permute-done.4.refs_1_ = bf16[64,1152]{1,0:T(8,128)(2,1)S(1)} collective-permute-done((bf16[64,1152]{1,0:T(8,128)(2,1)S(1)}, bf16[64,1152]{1,0:T(8,128)(2,1)S(1)}, u32[]{:S(2)}, u32[]{:S(2)}) %collective-permute-start.4) | collective-permute-done | bytes 147488 | tf_op jit(solution)/shard_map/ppermute | solution.py:430
  35.7 2.8 %collective-permute-start.12 = (bf16[8,32,512]{2,1,0:T(8,128)(2,1)S(1)}, bf16[8,32,512]{2,1,0:T(8,128)(2,1)S(1)}, u32[]{:S(2)}, u32[]{:S(2)}) collective-permute-start(bf16[8,32,512]{2,1,0:T(8,128)(2,1)S(1)} %get-tuple-element.57.refs_0_), channel_id=1, source_target_pairs={{0,2},{2,0},{4,6},{6,4},{1,3},{3,1},{5,7},{7,5},{8,10},{10,8},{12,... | collective-permute-start | bytes 786440 | tf_op jit(solution)/shard_map/ppermute | solution.py:461
  38.6 1.4 %collective-permute-start.16 = (bf16[8,32,512]{2,1,0:T(8,128)(2,1)S(1)}, bf16[8,32,512]{2,1,0:T(8,128)(2,1)S(1)}, u32[]{:S(2)}, u32[]{:S(2)}) collective-permute-start(bf16[8,32,512]{2,1,0:T(8,128)(2,1)S(1)} %get-tuple-element.59.refs_3_), channel_id=1, source_target_pairs={{0,8},{8,0},{16,24},{24,16},{1,9},{9,1},{17,25},{25,17},{2,10},{10... | collective-permute-start | bytes 786440 | tf_op jit(solution)/shard_map/ppermute | solution.py:406
  40.0 0.9 %collective-permute-start.17 = (bf16[8,32,512]{2,1,0:T(8,128)(2,1)S(1)}, bf16[8,32,512]{2,1,0:T(8,128)(2,1)S(1)}, u32[]{:S(2)}, u32[]{:S(2)}) collective-permute-start(bf16[8,32,512]{2,1,0:T(8,128)(2,1)S(1)} %get-tuple-element.59.refs_3_), channel_id=1, source_target_pairs={{0,16},{8,24},{16,0},{24,8},{1,17},{9,25},{17,1},{25,9},{2,18},{10... | collective-permute-start | bytes 786440 | tf_op jit(solution)/shard_map/ppermute | solution.py:406
  40.9 1.2 %collective-permute-start.18 = (bf16[8,32,512]{2,1,0:T(8,128)(2,1)S(1)}, bf16[8,32,512]{2,1,0:T(8,128)(2,1)S(1)}, u32[]{:S(2)}, u32[]{:S(2)}) collective-permute-start(bf16[8,32,512]{2,1,0:T(8,128)(2,1)S(1)} %get-tuple-element.59.refs_3_), channel_id=1, source_target_pairs={{0,24},{8,16},{16,8},{24,0},{1,25},{9,17},{17,9},{25,1},{2,26},{10... | collective-permute-start | bytes 786440 | tf_op jit(solution)/shard_map/ppermute | solution.py:406
  42.1 8.6 %collective-permute-done.13.refs_2_ = bf16[8,32,512]{2,1,0:T(8,128)(2,1)S(1)} collective-permute-done((bf16[8,32,512]{2,1,0:T(8,128)(2,1)S(1)}, bf16[8,32,512]{2,1,0:T(8,128)(2,1)S(1)}, u32[]{:S(2)}, u32[]{:S(2)}) %collective-permute-start.13) | collective-permute-done | bytes 262176 | tf_op jit(solution)/shard_map/ppermute | solution.py:461
  50.7 1.1 %collective-permute-done.17.refs_5_ = bf16[8,32,512]{2,1,0:T(8,128)(2,1)S(1)} collective-permute-done((bf16[8,32,512]{2,1,0:T(8,128)(2,1)S(1)}, bf16[8,32,512]{2,1,0:T(8,128)(2,1)S(1)}, u32[]{:S(2)}, u32[]{:S(2)}) %collective-permute-start.17) | collective-permute-done | bytes 262176 | tf_op jit(solution)/shard_map/ppermute | solution.py:406
  51.9 1.7 %collective-permute-done.18.refs_6_ = bf16[8,32,512]{2,1,0:T(8,128)(2,1)S(1)} collective-permute-done((bf16[8,32,512]{2,1,0:T(8,128)(2,1)S(1)}, bf16[8,32,512]{2,1,0:T(8,128)(2,1)S(1)}, u32[]{:S(2)}, u32[]{:S(2)}) %collective-permute-start.18) | collective-permute-done | bytes 262176 | tf_op jit(solution)/shard_map/ppermute | solution.py:406
  53.5 1.2 %near_square.1 = (f32[256,512]{1,0:T(8,128)S(1)}, bf16[4,256,256]{2,1,0:T(8,128)(2,1)S(1)}, bf16[1,256,512]{2,1,0:T(8,128)(2,1)S(1)}, bf16[3,4,32,512]{3,2,1,0:T(8,128)(2,1)S(1)}) custom-call(bf16[8,32,512]{2,1,0:T(8,128)(2,1)S(1)} %get-tuple-element.57.refs_0_, bf16[8,32,512]{2,1,0:T(8,128)(2,1)S(1)} %collective-permute-done.12.refs_1_, ...), custom_call_target="tpu_custom_call" | custom-call | tf_op jit(solution)/shard_map/near_square/pallas_call | solution.py:569
  55.8 3.0 %collective-permute-done.14.refs_0_.refs_7_.refs_3_ = bf16[8,32,512]{2,1,0:T(8,128)(2,1)S(1)} collective-permute-done((bf16[8,32,512]{2,1,0:T(8,128)(2,1)S(1)}, bf16[8,32,512]{2,1,0:T(8,128)(2,1)S(1)}, u32[]{:S(2)}, u32[]{:S(2)}) %collective-permute-start.14) | collective-permute-done | bytes 262176 | tf_op jit(solution)/shard_map/ppermute | solution.py:461
  58.8 0.7 far_square.1
  59.5 1.4 %collective-permute-start.24 = (bf16[8,32,512]{2,1,0:T(8,128)(2,1)S(1)}, bf16[8,32,512]{2,1,0:T(8,128)(2,1)S(1)}, u32[]{:S(2)}, u32[]{:S(2)}) collective-permute-start(bf16[8,32,512]{2,1,0:T(8,128)(2,1)S(1)} %get-tuple-element.68.refs_7_), channel_id=1, source_target_pairs={{0,16},{8,24},{16,0},{24,8},{1,17},{9,25},{17,1},{25,9},{2,18},{10... | collective-permute-start | bytes 786440 | tf_op jit(solution)/shard_map/ppermute | solution.py:471
  61.5 5.4 %collective-permute-done.24.refs_9_ = bf16[8,32,512]{2,1,0:T(8,128)(2,1)S(1)} collective-permute-done((bf16[8,32,512]{2,1,0:T(8,128)(2,1)S(1)}, bf16[8,32,512]{2,1,0:T(8,128)(2,1)S(1)}, u32[]{:S(2)}, u32[]{:S(2)}) %collective-permute-start.24) | collective-permute-done | bytes 262176 | tf_op jit(solution)/shard_map/ppermute | solution.py:471
  67.7 1.5 %collective-permute-start.27 = (bf16[4,32,512]{2,1,0:T(8,128)(2,1)S(1)}, bf16[4,32,512]{2,1,0:T(8,128)(2,1)S(1)}, u32[]{:S(2)}, u32[]{:S(2)}) collective-permute-start(bf16[4,32,512]{2,1,0:T(8,128)(2,1)S(1)} %slice.9), channel_id=1, source_target_pairs={{0,16},{8,24},{16,0},{24,8},{1,17},{9,25},{17,1},{25,9},{2,18},{10... | collective-permute-start | bytes 393224 | tf_op jit(solution)/shard_map/ppermute | solution.py:475
  69.7 2.2 %collective-permute-done.26.refs_10_.refs_0_ = bf16[4,32,512]{2,1,0:T(8,128)(2,1)S(1)} collective-permute-done((bf16[4,32,512]{2,1,0:T(8,128)(2,1)S(1)}, bf16[4,32,512]{2,1,0:T(8,128)(2,1)S(1)}, u32[]{:S(2)}, u32[]{:S(2)}) %collective-permute-start.26) | collective-permute-done | bytes 131104 | tf_op jit(solution)/shard_map/ppermute | solution.py:474
  71.9 0.8 %collective-permute-done.27.refs_11_.refs_1_ = bf16[4,32,512]{2,1,0:T(8,128)(2,1)S(1)} collective-permute-done((bf16[4,32,512]{2,1,0:T(8,128)(2,1)S(1)}, bf16[4,32,512]{2,1,0:T(8,128)(2,1)S(1)}, u32[]{:S(2)}, u32[]{:S(2)}) %collective-permute-start.27) | collective-permute-done | bytes 131104 | tf_op jit(solution)/shard_map/ppermute | solution.py:475
  72.8 1.3 %near_cube.1 = (f32[256,512]{1,0:T(8,128)S(1)}, bf16[256,512]{1,0:T(8,128)(2,1)S(1)}, bf16[256,256]{1,0:T(8,128)(2,1)S(1)}) custom-call(bf16[8,32,512]{2,1,0:T(8,128)(2,1)S(1)} %get-tuple-element.57.refs_0_, bf16[8,32,512]{2,1,0:T(8,128)(2,1)S(1)} %collective-permute-done.12.refs_1_, bf16[8,32,512]{2,1,0:T(8,128)(2,1)S(1)} %collective-permute-done.13.refs_2_, ...), custom_call_target="tpu_custom_call" | custom-call | tf_op jit(solution)/shard_map/near_cube/pallas_call | solution.py:606
  74.2 1.0 %far_cube.1 = f32[256,512]{1,0:T(8,128)} custom-call(f32[256,512]{1,0:T(8,128)S(1)} %get-tuple-element.72.sum_ref, bf16[256,512]{1,0:T(8,128)(2,1)S(1)} %get-tuple-element.73.mask_ref, bf16[256,256]{1,0:T(8,128)(2,1)S(1)} %get-tuple-element.74.left_ref, bf16[4,32,512]{2,1,0:T(8,128)(2,1)S(1)} %collective-permute-done.31.refs_0_, ...), custom_call_target="tpu_custom_call" | custom-call | flops 268435456 | bytes 4194304 | tf_op jit(solution)/shard_map/far_cube/pallas_call | solution.py:624
  (58 shorter events, 5.9 us)
Async XLA Ops:
  2.2 8.9 %collective-permute-start.6 = (bf16[64,1024]{1,0:T(8,128)(2,1)S(1)}, bf16[64,1024]{1,0:T(8,128)(2,1)S(1)}, u32[]{:S(2)}, u32[]{:S(2)}) collective-permute-start(bf16[64,1024]{1,0:T(8,128)(2,1)S(1)} %get-tuple-element.49), channel_id=1, source_target_pairs={{0,2},{2,0},{4,6},{6,4},{1,3},{3,1},{5,7},{7,5},{8,10},{10,8},{12,... | collective-permute-start | bytes 393224 | tf_op jit(solution)/shard_map/ppermute | solution.py:414
  5.3 12.9 %collective-permute-start.7 = (bf16[64,1024]{1,0:T(8,128)(2,1)S(1)}, bf16[64,1024]{1,0:T(8,128)(2,1)S(1)}, u32[]{:S(2)}, u32[]{:S(2)}) collective-permute-start(bf16[64,1024]{1,0:T(8,128)(2,1)S(1)} %get-tuple-element.50), channel_id=1, source_target_pairs={{0,4},{2,6},{4,0},{6,2},{1,5},{3,7},{5,1},{7,3},{8,12},{10,14},{12... | collective-permute-start | bytes 393224 | tf_op jit(solution)/shard_map/ppermute | solution.py:414
  7.9 10.3 %collective-permute-start.8 = (bf16[64,1024]{1,0:T(8,128)(2,1)S(1)}, bf16[64,1024]{1,0:T(8,128)(2,1)S(1)}, u32[]{:S(2)}, u32[]{:S(2)}) collective-permute-start(bf16[64,1024]{1,0:T(8,128)(2,1)S(1)} %get-tuple-element.51), channel_id=1, source_target_pairs={{0,6},{2,4},{4,2},{6,0},{1,7},{3,5},{5,3},{7,1},{8,14},{10,12},{12... | collective-permute-start | bytes 393224 | tf_op jit(solution)/shard_map/ppermute | solution.py:414
  7.9 11.9 %collective-permute-start = (bf16[64,1152]{1,0:T(8,128)(2,1)S(1)}, bf16[64,1152]{1,0:T(8,128)(2,1)S(1)}, u32[]{:S(2)}, u32[]{:S(2)}) collective-permute-start(bf16[64,1152]{1,0:T(8,128)(2,1)S(1)} %get-tuple-element.40), channel_id=1, source_target_pairs={{0,24},{8,16},{16,8},{24,0},{1,25},{9,17},{17,9},{25,1},{2,26},{10... | collective-permute-start | bytes 442376 | tf_op jit(solution)/shard_map/ppermute | solution.py:414
  10.5 9.3 %collective-permute-start.1 = (bf16[64,1152]{1,0:T(8,128)(2,1)S(1)}, bf16[64,1152]{1,0:T(8,128)(2,1)S(1)}, u32[]{:S(2)}, u32[]{:S(2)}) collective-permute-start(bf16[64,1152]{1,0:T(8,128)(2,1)S(1)} %get-tuple-element.41), channel_id=1, source_target_pairs={{0,16},{8,24},{16,0},{24,8},{1,17},{9,25},{17,1},{25,9},{2,18},{10... | collective-permute-start | bytes 442376 | tf_op jit(solution)/shard_map/ppermute | solution.py:414
  11.0 8.8 %collective-permute-start.2 = (bf16[64,1152]{1,0:T(8,128)(2,1)S(1)}, bf16[64,1152]{1,0:T(8,128)(2,1)S(1)}, u32[]{:S(2)}, u32[]{:S(2)}) collective-permute-start(bf16[64,1152]{1,0:T(8,128)(2,1)S(1)} %get-tuple-element.42), channel_id=1, source_target_pairs={{0,8},{8,0},{16,24},{24,16},{1,9},{9,1},{17,25},{25,17},{2,10},{10... | collective-permute-start | bytes 442376 | tf_op jit(solution)/shard_map/ppermute | solution.py:414
  18.2 7.6 %collective-permute-start.9 = (bf16[64,1024]{1,0:T(8,128)(2,1)S(1)}, bf16[64,1024]{1,0:T(8,128)(2,1)S(1)}, u32[]{:S(2)}, u32[]{:S(2)}) collective-permute-start(bf16[64,1024]{1,0:T(8,128)(2,1)S(1)} %get-tuple-element.52), channel_id=1, source_target_pairs={{0,8},{8,0},{16,24},{24,16},{1,9},{9,1},{17,25},{25,17},{2,10},{10... | collective-permute-start | bytes 393224 | tf_op jit(solution)/shard_map/ppermute | solution.py:430
  19.8 11.9 %collective-permute-start.3 = (bf16[64,1152]{1,0:T(8,128)(2,1)S(1)}, bf16[64,1152]{1,0:T(8,128)(2,1)S(1)}, u32[]{:S(2)}, u32[]{:S(2)}) collective-permute-start(bf16[64,1152]{1,0:T(8,128)(2,1)S(1)} %get-tuple-element.44), channel_id=1, source_target_pairs={{0,6},{2,4},{4,2},{6,0},{1,7},{3,5},{5,3},{7,1},{8,14},{10,12},{12... | collective-permute-start | bytes 442376 | tf_op jit(solution)/shard_map/ppermute | solution.py:430
  22.2 11.8 %collective-permute-start.4 = (bf16[64,1152]{1,0:T(8,128)(2,1)S(1)}, bf16[64,1152]{1,0:T(8,128)(2,1)S(1)}, u32[]{:S(2)}, u32[]{:S(2)}) collective-permute-start(bf16[64,1152]{1,0:T(8,128)(2,1)S(1)} %get-tuple-element.45), channel_id=1, source_target_pairs={{0,4},{2,6},{4,0},{6,2},{1,5},{3,7},{5,1},{7,3},{8,12},{10,14},{12... | collective-permute-start | bytes 442376 | tf_op jit(solution)/shard_map/ppermute | solution.py:430
  23.3 10.7 %collective-permute-start.5 = (bf16[64,1152]{1,0:T(8,128)(2,1)S(1)}, bf16[64,1152]{1,0:T(8,128)(2,1)S(1)}, u32[]{:S(2)}, u32[]{:S(2)}) collective-permute-start(bf16[64,1152]{1,0:T(8,128)(2,1)S(1)} %get-tuple-element.46), channel_id=1, source_target_pairs={{0,2},{2,0},{4,6},{6,4},{1,3},{3,1},{5,7},{7,5},{8,10},{10,8},{12,... | collective-permute-start | bytes 442376 | tf_op jit(solution)/shard_map/ppermute | solution.py:430
  24.3 5.0 %collective-permute-start.10 = (bf16[64,1024]{1,0:T(8,128)(2,1)S(1)}, bf16[64,1024]{1,0:T(8,128)(2,1)S(1)}, u32[]{:S(2)}, u32[]{:S(2)}) collective-permute-start(bf16[64,1024]{1,0:T(8,128)(2,1)S(1)} %get-tuple-element.53), channel_id=1, source_target_pairs={{0,16},{8,24},{16,0},{24,8},{1,17},{9,25},{17,1},{25,9},{2,18},{10... | collective-permute-start | bytes 393224 | tf_op jit(solution)/shard_map/ppermute | solution.py:430
  25.8 5.9 %collective-permute-start.11 = (bf16[64,1024]{1,0:T(8,128)(2,1)S(1)}, bf16[64,1024]{1,0:T(8,128)(2,1)S(1)}, u32[]{:S(2)}, u32[]{:S(2)}) collective-permute-start(bf16[64,1024]{1,0:T(8,128)(2,1)S(1)} %get-tuple-element.54), channel_id=1, source_target_pairs={{0,24},{8,16},{16,8},{24,0},{1,25},{9,17},{17,9},{25,1},{2,26},{10... | collective-permute-start | bytes 393224 | tf_op jit(solution)/shard_map/ppermute | solution.py:430
  35.2 3.4 %collective-permute-start.15 = (bf16[8,32,512]{2,1,0:T(8,128)(2,1)S(1)}, bf16[8,32,512]{2,1,0:T(8,128)(2,1)S(1)}, u32[]{:S(2)}, u32[]{:S(2)}) collective-permute-start(bf16[8,32,512]{2,1,0:T(8,128)(2,1)S(1)} %get-tuple-element.59.refs_3_), channel_id=1, source_target_pairs={{0,1},{1,0},{2,3},{3,2},{4,5},{5,4},{6,7},{7,6},{8,9},{9,8},{10,11... | collective-permute-start | bytes 786440 | tf_op jit(solution)/shard_map/ppermute | solution.py:481
  35.3 15.3 %collective-permute-start.13 = (bf16[8,32,512]{2,1,0:T(8,128)(2,1)S(1)}, bf16[8,32,512]{2,1,0:T(8,128)(2,1)S(1)}, u32[]{:S(2)}, u32[]{:S(2)}) collective-permute-start(bf16[8,32,512]{2,1,0:T(8,128)(2,1)S(1)} %get-tuple-element.57.refs_0_), channel_id=1, source_target_pairs={{0,4},{2,6},{4,0},{6,2},{1,5},{3,7},{5,1},{7,3},{8,12},{10,14},{12... | collective-permute-start | bytes 786440 | tf_op jit(solution)/shard_map/ppermute | solution.py:461
  35.7 15.0 %collective-permute-start.12 = (bf16[8,32,512]{2,1,0:T(8,128)(2,1)S(1)}, bf16[8,32,512]{2,1,0:T(8,128)(2,1)S(1)}, u32[]{:S(2)}, u32[]{:S(2)}) collective-permute-start(bf16[8,32,512]{2,1,0:T(8,128)(2,1)S(1)} %get-tuple-element.57.refs_0_), channel_id=1, source_target_pairs={{0,2},{2,0},{4,6},{6,4},{1,3},{3,1},{5,7},{7,5},{8,10},{10,8},{12,... | collective-permute-start | bytes 786440 | tf_op jit(solution)/shard_map/ppermute | solution.py:461
  38.6 12.1 %collective-permute-start.16 = (bf16[8,32,512]{2,1,0:T(8,128)(2,1)S(1)}, bf16[8,32,512]{2,1,0:T(8,128)(2,1)S(1)}, u32[]{:S(2)}, u32[]{:S(2)}) collective-permute-start(bf16[8,32,512]{2,1,0:T(8,128)(2,1)S(1)} %get-tuple-element.59.refs_3_), channel_id=1, source_target_pairs={{0,8},{8,0},{16,24},{24,16},{1,9},{9,1},{17,25},{25,17},{2,10},{10... | collective-permute-start | bytes 786440 | tf_op jit(solution)/shard_map/ppermute | solution.py:406
  40.0 11.8 %collective-permute-start.17 = (bf16[8,32,512]{2,1,0:T(8,128)(2,1)S(1)}, bf16[8,32,512]{2,1,0:T(8,128)(2,1)S(1)}, u32[]{:S(2)}, u32[]{:S(2)}) collective-permute-start(bf16[8,32,512]{2,1,0:T(8,128)(2,1)S(1)} %get-tuple-element.59.refs_3_), channel_id=1, source_target_pairs={{0,16},{8,24},{16,0},{24,8},{1,17},{9,25},{17,1},{25,9},{2,18},{10... | collective-permute-start | bytes 786440 | tf_op jit(solution)/shard_map/ppermute | solution.py:406
  40.9 12.6 %collective-permute-start.18 = (bf16[8,32,512]{2,1,0:T(8,128)(2,1)S(1)}, bf16[8,32,512]{2,1,0:T(8,128)(2,1)S(1)}, u32[]{:S(2)}, u32[]{:S(2)}) collective-permute-start(bf16[8,32,512]{2,1,0:T(8,128)(2,1)S(1)} %get-tuple-element.59.refs_3_), channel_id=1, source_target_pairs={{0,24},{8,16},{16,8},{24,0},{1,25},{9,17},{17,9},{25,1},{2,26},{10... | collective-permute-start | bytes 786440 | tf_op jit(solution)/shard_map/ppermute | solution.py:406
  50.6 8.2 %collective-permute-start.14 = (bf16[8,32,512]{2,1,0:T(8,128)(2,1)S(1)}, bf16[8,32,512]{2,1,0:T(8,128)(2,1)S(1)}, u32[]{:S(2)}, u32[]{:S(2)}) collective-permute-start(bf16[8,32,512]{2,1,0:T(8,128)(2,1)S(1)} %collective-permute-done.13.refs_2_), channel_id=1, source_target_pairs={{0,2},{2,0},{4,6},{6,4},{1,3},{3,1},{5,7},{7,5},{8,10},{10,8},{12,... | collective-permute-start | bytes 786440 | tf_op jit(solution)/shard_map/ppermute | solution.py:461
  54.7 4.1 %collective-permute-start.19 = (bf16[3,4,32,512]{3,2,1,0:T(8,128)(2,1)S(1)}, bf16[3,4,32,512]{3,2,1,0:T(8,128)(2,1)S(1)}, u32[]{:S(2)}, u32[]{:S(2)}) collective-permute-start(bf16[3,4,32,512]{3,2,1,0:T(8,128)(2,1)S(1)} %get-tuple-element.60), channel_id=1, source_target_pairs={{0,1},{1,0},{2,3},{3,2},{4,5},{5,4},{6,7},{7,6},{8,9},{9,8},{10,11... | collective-permute-start | bytes 1179656 | tf_op jit(solution)/shard_map/ppermute | solution.py:481
  54.8 4.0 %collective-permute-start.20 = (bf16[8,32,512]{2,1,0:T(8,128)(2,1)S(1)}, bf16[8,32,512]{2,1,0:T(8,128)(2,1)S(1)}, u32[]{:S(2)}, u32[]{:S(2)}) collective-permute-start(bf16[8,32,512]{2,1,0:T(8,128)(2,1)S(1)} %collective-permute-done.16.refs_4_), channel_id=1, source_target_pairs={{0,1},{1,0},{2,3},{3,2},{4,5},{5,4},{6,7},{7,6},{8,9},{9,8},{10,11... | collective-permute-start | bytes 786440 | tf_op jit(solution)/shard_map/ppermute | solution.py:481
  55.3 3.5 %collective-permute-start.21 = (bf16[8,32,512]{2,1,0:T(8,128)(2,1)S(1)}, bf16[8,32,512]{2,1,0:T(8,128)(2,1)S(1)}, u32[]{:S(2)}, u32[]{:S(2)}) collective-permute-start(bf16[8,32,512]{2,1,0:T(8,128)(2,1)S(1)} %collective-permute-done.17.refs_5_), channel_id=1, source_target_pairs={{0,1},{1,0},{2,3},{3,2},{4,5},{5,4},{6,7},{7,6},{8,9},{9,8},{10,11... | collective-permute-start | bytes 786440 | tf_op jit(solution)/shard_map/ppermute | solution.py:481
  55.3 3.4 %collective-permute-start.22 = (bf16[8,32,512]{2,1,0:T(8,128)(2,1)S(1)}, bf16[8,32,512]{2,1,0:T(8,128)(2,1)S(1)}, u32[]{:S(2)}, u32[]{:S(2)}) collective-permute-start(bf16[8,32,512]{2,1,0:T(8,128)(2,1)S(1)} %collective-permute-done.18.refs_6_), channel_id=1, source_target_pairs={{0,1},{1,0},{2,3},{3,2},{4,5},{5,4},{6,7},{7,6},{8,9},{9,8},{10,11... | collective-permute-start | bytes 786440 | tf_op jit(solution)/shard_map/ppermute | solution.py:481
  59.5 7.4 %collective-permute-start.24 = (bf16[8,32,512]{2,1,0:T(8,128)(2,1)S(1)}, bf16[8,32,512]{2,1,0:T(8,128)(2,1)S(1)}, u32[]{:S(2)}, u32[]{:S(2)}) collective-permute-start(bf16[8,32,512]{2,1,0:T(8,128)(2,1)S(1)} %get-tuple-element.68.refs_7_), channel_id=1, source_target_pairs={{0,16},{8,24},{16,0},{24,8},{1,17},{9,25},{17,1},{25,9},{2,18},{10... | collective-permute-start | bytes 786440 | tf_op jit(solution)/shard_map/ppermute | solution.py:471
  60.9 6.8 %collective-permute-start.23 = (bf16[8,32,512]{2,1,0:T(8,128)(2,1)S(1)}, bf16[8,32,512]{2,1,0:T(8,128)(2,1)S(1)}, u32[]{:S(2)}, u32[]{:S(2)}) collective-permute-start(bf16[8,32,512]{2,1,0:T(8,128)(2,1)S(1)} %get-tuple-element.68.refs_7_), channel_id=1, source_target_pairs={{0,8},{8,0},{16,24},{24,16},{1,9},{9,1},{17,25},{25,17},{2,10},{10... | collective-permute-start | bytes 786440 | tf_op jit(solution)/shard_map/ppermute | solution.py:471
  61.5 8.2 %collective-permute-start.28 = (bf16[8,32,512]{2,1,0:T(8,128)(2,1)S(1)}, bf16[8,32,512]{2,1,0:T(8,128)(2,1)S(1)}, u32[]{:S(2)}, u32[]{:S(2)}) collective-permute-start(bf16[8,32,512]{2,1,0:T(8,128)(2,1)S(1)} %get-tuple-element.68.refs_7_), channel_id=1, source_target_pairs={{0,1},{1,0},{2,3},{3,2},{4,5},{5,4},{6,7},{7,6},{8,9},{9,8},{10,11... | collective-permute-start | bytes 786440 | tf_op jit(solution)/shard_map/ppermute | solution.py:481
  66.9 5.0 %collective-permute-start.26 = (bf16[4,32,512]{2,1,0:T(8,128)(2,1)S(1)}, bf16[4,32,512]{2,1,0:T(8,128)(2,1)S(1)}, u32[]{:S(2)}, u32[]{:S(2)}) collective-permute-start(bf16[4,32,512]{2,1,0:T(8,128)(2,1)S(1)} %slice.8), channel_id=1, source_target_pairs={{0,8},{8,0},{16,24},{24,16},{1,9},{9,1},{17,25},{25,17},{2,10},{10... | collective-permute-start | bytes 393224 | tf_op jit(solution)/shard_map/ppermute | solution.py:474
  67.7 5.0 %collective-permute-start.27 = (bf16[4,32,512]{2,1,0:T(8,128)(2,1)S(1)}, bf16[4,32,512]{2,1,0:T(8,128)(2,1)S(1)}, u32[]{:S(2)}, u32[]{:S(2)}) collective-permute-start(bf16[4,32,512]{2,1,0:T(8,128)(2,1)S(1)} %slice.9), channel_id=1, source_target_pairs={{0,16},{8,24},{16,0},{24,8},{1,17},{9,25},{17,1},{25,9},{2,18},{10... | collective-permute-start | bytes 393224 | tf_op jit(solution)/shard_map/ppermute | solution.py:475
  69.2 3.6 %collective-permute-start.25 = (bf16[4,32,512]{2,1,0:T(8,128)(2,1)S(1)}, bf16[4,32,512]{2,1,0:T(8,128)(2,1)S(1)}, u32[]{:S(2)}, u32[]{:S(2)}) collective-permute-start(bf16[4,32,512]{2,1,0:T(8,128)(2,1)S(1)} %get-tuple-element.69), channel_id=1, source_target_pairs={{0,1},{1,0},{2,3},{3,2},{4,5},{5,4},{6,7},{7,6},{8,9},{9,8},{10,11... | collective-permute-start | bytes 393224 | tf_op jit(solution)/shard_map/ppermute | solution.py:481
  69.2 3.6 %collective-permute-start.29 = (bf16[8,32,512]{2,1,0:T(8,128)(2,1)S(1)}, bf16[8,32,512]{2,1,0:T(8,128)(2,1)S(1)}, u32[]{:S(2)}, u32[]{:S(2)}) collective-permute-start(bf16[8,32,512]{2,1,0:T(8,128)(2,1)S(1)} %collective-permute-done.23.refs_8_), channel_id=1, source_target_pairs={{0,1},{1,0},{2,3},{3,2},{4,5},{5,4},{6,7},{7,6},{8,9},{9,8},{10,11... | collective-permute-start | bytes 786440 | tf_op jit(solution)/shard_map/ppermute | solution.py:481
  69.7 3.1 %collective-permute-start.30 = (bf16[8,32,512]{2,1,0:T(8,128)(2,1)S(1)}, bf16[8,32,512]{2,1,0:T(8,128)(2,1)S(1)}, u32[]{:S(2)}, u32[]{:S(2)}) collective-permute-start(bf16[8,32,512]{2,1,0:T(8,128)(2,1)S(1)} %collective-permute-done.24.refs_9_), channel_id=1, source_target_pairs={{0,1},{1,0},{2,3},{3,2},{4,5},{5,4},{6,7},{7,6},{8,9},{9,8},{10,11... | collective-permute-start | bytes 786440 | tf_op jit(solution)/shard_map/ppermute | solution.py:481
  71.9 2.2 %collective-permute-start.31 = (bf16[4,32,512]{2,1,0:T(8,128)(2,1)S(1)}, bf16[4,32,512]{2,1,0:T(8,128)(2,1)S(1)}, u32[]{:S(2)}, u32[]{:S(2)}) collective-permute-start(bf16[4,32,512]{2,1,0:T(8,128)(2,1)S(1)} %collective-permute-done.26.refs_10_.refs_0_), channel_id=1, source_target_pairs={{0,1},{1,0},{2,3},{3,2},{4,5},{5,4},{6,7},{7,6},{8,9},{9,8},{10,11... | collective-permute-start | bytes 393224 | tf_op jit(solution)/shard_map/ppermute | solution.py:481
  (6 other events, 11.0 us)
